TPU v7x, 256 devices: a whole 4x4x8 slice. The times are simulated.
256 devices in a mesh: sect: 4 (over z_hi, core), ctx: 4 (over z_lo), tp: 16 (over y, x).
Axes of the slice: x: 4, y: 4, z: 8 (z_hi: 2, z_lo: 4; z = z_hi * 4 + z_lo), core: 2. Of those that a mesh axis runs over, the one named last changes fastest.
Arguments:
- span_queries: bfloat16 [4, 256, 8192], P('sect', 'ctx', 'tp'), may hold values from -15 to 15
- prompt_cache: bfloat16 [4, 2, 16384, 1024], P('sect', None, ('ctx', 'tp')), may hold values from -6 to 6
- span_kv: bfloat16 [4, 2, 256, 1024], P('sect', None, ('ctx', 'tp')), may hold values from -6 to 6
- span_offsets: int32 [4], P('sect'), may hold values from 0 to 16384, as said below
- decode_queries: bfloat16 [64, 8192], P(('sect', 'ctx'), 'tp'), may hold values from -12.5 to 12.5
- decode_cache: bfloat16 [64, 2, 2048, 1024], P(('sect', 'ctx'), None, 'tp'), may hold values from -6 to 6
- cache_lengths: int32 [64], P(('sect', 'ctx')), may hold values from 1 to 2048, as said below
- owner_rows: int32 [4], replicated, may hold values from 0 to 63, as said below
Outputs:
- span_attention: bfloat16 [4, 256, 8192], P('sect', 'ctx', 'tp')
- decode_attention: bfloat16 [64, 8192], P(('sect', 'ctx'), 'tp')
Inputs may be any that keep to these rules, and one draw needn't show every extreme that they name: `span_offsets`: some request has exactly 16384. `cache_lengths`: some row has exactly 2048. `owner_rows`: all entries differ; some request goes to row 63.
All inputs are finite; a program needn't handle non-finite values.
Results may differ from a plain program's by a relative error of at most 0.0075.
Values may be sent and summed in bfloat16 or wider, within the bound.
A program may use at most 128 MiB of HBM per device.

v0:
```python
import math

import jax
import jax.numpy as jnp
from jax import lax
from jax.sharding import PartitionSpec as P

Q_HEADS = 64
KV_HEADS = 8
HEAD_DIM = 128


masked_score = -1e30


def merged(x, axis, combine):
    everything = jax.tree.map(lambda part: lax.all_gather(part, axis), x)
    leading = jax.tree.map(lambda part: part[0], everything)

    def hop(k, so_far):
        return combine(so_far, jax.tree.map(lambda part: part[k], everything))

    return lax.fori_loop(1, lax.axis_size(axis), hop, leading)


def join_pair(former, latter):
    overall = jnp.maximum(former[0], latter[0])
    left_factor = jnp.exp(former[0] - overall)
    right_factor = jnp.exp(latter[0] - overall)
    return (
        overall,
        former[1] * left_factor + latter[1] * right_factor,
        former[2] * left_factor[..., None] + latter[2] * right_factor[..., None],
    )


def fold_parts(maxima, totals, sums, stack_dim):
    overall = jnp.max(maxima, axis=stack_dim, keepdims=True)
    factor = jnp.exp(maxima - overall)
    combined = jnp.sum(sums * factor[..., None], axis=stack_dim)
    return combined / jnp.sum(totals * factor, axis=stack_dim)[..., None]


def partial_block(queries, key_rows, value_rows, visible):
    score_scale = 1.0 / math.sqrt(HEAD_DIM)
    scores = (
        jnp.einsum("tkgd,pkd->tkgp", queries, key_rows, preferred_element_type=jnp.float32)
        * score_scale
    )
    allowed = visible[:, None, None, :]
    scores = jnp.where(allowed, scores, masked_score)
    row_max = jnp.max(scores, axis=-1)
    weights = jnp.where(allowed, jnp.exp(scores - row_max[..., None]), 0.0)
    row_sum = jnp.sum(weights, axis=-1)
    weighted = jnp.einsum(
        "tkgp,pkd->tkgd",
        weights.astype(jnp.bfloat16),
        value_rows,
        preferred_element_type=jnp.float32,
    )
    return (row_max, row_sum, weighted)


def spread_positions(span_queries, prompt_cache, span_kv, offset):
    tp_count = lax.axis_size("tp")
    ctx_count = lax.axis_size("ctx")
    block_index = lax.axis_index("ctx") * tp_count + lax.axis_index("tp")
    block_count = ctx_count * tp_count
    tok_local = span_queries.shape[1]
    head_local = span_queries.shape[2] // HEAD_DIM
    group_size = Q_HEADS // KV_HEADS
    prompt_count = prompt_cache.shape[2]
    span_count = span_kv.shape[2]
    span_total = tok_local * ctx_count
    gathered = lax.all_gather(span_queries, ("ctx", "tp"), axis=0, tiled=True)
    queries = gathered.reshape(ctx_count, tp_count, tok_local, head_local, HEAD_DIM).transpose(
        0, 2, 1, 3, 4
    )
    queries = queries.reshape(span_total, KV_HEADS, 1, group_size, HEAD_DIM).transpose(
        1, 0, 2, 3, 4
    )

    def head_major(tensor, position_count):
        return tensor.reshape(position_count, KV_HEADS, 1, HEAD_DIM).transpose(1, 0, 2, 3)

    prompt_keys = head_major(prompt_cache[0, 0], prompt_count)
    prompt_values = head_major(prompt_cache[0, 1], prompt_count)
    span_keys = head_major(span_kv[0, 0], span_count)
    span_values = head_major(span_kv[0, 1], span_count)
    positions = block_index * prompt_count + jnp.arange(prompt_count)
    prompt_visible = jnp.broadcast_to((positions < offset)[None, :], (span_total, prompt_count))
    span_ids = block_index * span_count + jnp.arange(span_count)
    span_visible = span_ids[None, :] <= jnp.arange(span_total)[:, None]

    def one_head(pieces):
        query_head, prompt_key, prompt_value, span_key, span_value = pieces
        former = partial_block(query_head, prompt_key, prompt_value, prompt_visible)
        return join_pair(former, partial_block(query_head, span_key, span_value, span_visible))

    row_max, row_sum, weighted = lax.map(
        one_head, (queries, prompt_keys, prompt_values, span_keys, span_values)
    )

    def to_blocks(tensor, width):
        ordered = tensor.reshape(KV_HEADS, span_total, group_size * width).transpose(1, 0, 2)
        ordered = ordered.reshape(ctx_count, tok_local, tp_count, head_local * width).transpose(
            0, 2, 1, 3
        )
        return ordered.reshape(block_count, tok_local, head_local * width)

    received = (
        lax.all_to_all(
            to_blocks(weighted, HEAD_DIM), ("ctx", "tp"), split_axis=0, concat_axis=0, tiled=True
        ),
        lax.all_to_all(
            to_blocks(row_max, 1), ("ctx", "tp"), split_axis=0, concat_axis=0, tiled=True
        ),
        lax.all_to_all(
            to_blocks(row_sum, 1), ("ctx", "tp"), split_axis=0, concat_axis=0, tiled=True
        ),
    )
    result = fold_parts(
        received[1],
        received[2],
        received[0].reshape(block_count, tok_local, head_local, HEAD_DIM),
        0,
    )
    return result.reshape(1, tok_local, head_local * HEAD_DIM).astype(jnp.bfloat16)


def decode_step(decode_queries, decode_cache, cache_lengths, span_kv, owner_rows):
    tp_count = lax.axis_size("tp")
    ctx_count = lax.axis_size("ctx")
    tp_index = lax.axis_index("tp")
    group_size = Q_HEADS // KV_HEADS
    score_scale = 1.0 / math.sqrt(HEAD_DIM)
    row_count = decode_queries.shape[0]
    head_local = decode_queries.shape[1] // HEAD_DIM
    cache_count = decode_cache.shape[2]
    gathered = lax.all_gather(decode_queries[:, None, :], "tp", axis=1, tiled=True)
    queries = gathered.reshape(row_count, KV_HEADS, group_size, HEAD_DIM)
    arrived = lax.all_gather(span_kv, ("sect", "ctx"), axis=0, tiled=True)
    per_block = arrived.shape[2]
    new_count = arrived.shape[0] * per_block
    new_keys = arrived[:, 0].reshape(new_count, KV_HEADS, HEAD_DIM)
    new_values = arrived[:, 1].reshape(new_count, KV_HEADS, HEAD_DIM)
    request_ids = jnp.arange(new_count) // (per_block * ctx_count)
    request_count = owner_rows.shape[0]
    key_owner = jnp.sum(
        jnp.where(
            request_ids[:, None] == jnp.arange(request_count)[None, :], owner_rows[None, :], 0
        ),
        axis=1,
    )
    group_id = lax.axis_index("sect") * ctx_count + lax.axis_index("ctx")
    row_ids = group_id * row_count + jnp.arange(row_count)
    new_visible = (key_owner[None, :] == row_ids[:, None])[:, None, None, :]
    positions = tp_index * cache_count + jnp.arange(cache_count)
    cache_visible = (positions[None, :] < cache_lengths[:, None])[:, None, None, :]
    cache_keys = decode_cache[:, 0].reshape(row_count, cache_count, KV_HEADS, HEAD_DIM)
    cache_values = decode_cache[:, 1].reshape(row_count, cache_count, KV_HEADS, HEAD_DIM)
    cache_scores = (
        jnp.einsum("rkgd,rpkd->rkgp", queries, cache_keys, preferred_element_type=jnp.float32)
        * score_scale
    )
    cache_scores = jnp.where(cache_visible, cache_scores, masked_score)
    new_scores = (
        jnp.einsum("rkgd,pkd->rkgp", queries, new_keys, preferred_element_type=jnp.float32)
        * score_scale
    )
    new_scores = jnp.where(new_visible, new_scores, masked_score)
    row_max = jnp.maximum(jnp.max(cache_scores, axis=-1), jnp.max(new_scores, axis=-1))
    cache_weights = jnp.where(cache_visible, jnp.exp(cache_scores - row_max[..., None]), 0.0)
    new_weights = jnp.where(new_visible, jnp.exp(new_scores - row_max[..., None]), 0.0)
    row_sum = jnp.sum(cache_weights, axis=-1) + jnp.sum(new_weights, axis=-1)
    weighted = jnp.einsum(
        "rkgp,rpkd->rkgd",
        cache_weights.astype(jnp.bfloat16),
        cache_values,
        preferred_element_type=jnp.float32,
    )
    weighted = weighted + jnp.einsum(
        "rkgp,pkd->rkgd",
        new_weights.astype(jnp.bfloat16),
        new_values,
        preferred_element_type=jnp.float32,
    )
    row_max, row_sum, weighted = merged((row_max, row_sum, weighted), "tp", join_pair)
    own_sum = lax.dynamic_index_in_dim(
        weighted.reshape(row_count, tp_count, head_local, HEAD_DIM), tp_index, 1, keepdims=False
    )
    own_total = lax.dynamic_index_in_dim(
        row_sum.reshape(row_count, tp_count, head_local), tp_index, 1, keepdims=False
    )
    result = own_sum / own_total[..., None]
    return result.reshape(row_count, head_local * HEAD_DIM).astype(jnp.bfloat16)


def body(
    span_queries,
    prompt_cache,
    span_kv,
    span_offsets,
    decode_queries,
    decode_cache,
    cache_lengths,
    owner_rows,
):
    offset = span_offsets[0]
    span_attention = spread_positions(span_queries, prompt_cache, span_kv, offset)
    decode_attention = decode_step(decode_queries, decode_cache, cache_lengths, span_kv, owner_rows)
    return (span_attention, decode_attention)


def solution(mesh):
    return jax.shard_map(
        body,
        mesh=mesh,
        in_specs=(
            P("sect", "ctx", "tp"),
            P("sect", None, ("ctx", "tp"), None),
            P("sect", None, ("ctx", "tp"), None),
            P("sect"),
            P(("sect", "ctx"), "tp"),
            P(("sect", "ctx"), None, "tp", None),
            P(("sect", "ctx")),
            P(),
        ),
        out_specs=(P("sect", "ctx", "tp"), P(("sect", "ctx"), "tp")),
        check_vma=False,
    )
```

profile of v0, /device:TPU:2, one launch (start us, length us, event | category | flops | bytes accessed | tf_op | source)
XLA Modules:
  0.0 790.6 jit_solution(8635588638938088984)
XLA Ops:
  8.8 1.3 fusion.82
  11.2 355.2 %all-gather.7.cloned.1.call-done = bf16[64,64,512]{2,1,0:T(8,128)(2,1)} async-done(((bf16[1,64,512]{2,1,0:T(8,128)(2,1)}), bf16[64,64,512]{2,1,0:T(8,128)(2,1)}) %all-gather.7.cloned.1.call-update) | async-done | bytes 4194320 | tf_op jit(solution)/shard_map/all_gather | solution.py:75
  366.4 6.9 reshape.331
  373.3 5.3 copy.110
  378.6 45.6 %while.35 = (s32[]{:T(128)}, f32[8,256,1,8]{1,3,2,0:T(8,128)S(1)}, f32[8,256,1,8]{1,3,2,0:T(8,128)S(1)}, f32[8,256,1,8,128]{1,4,3,2,0:T(8,128)}, bf16[8,256,1,12...) while((s32[]{:T(128)}, f32[8,256,1,8]{1,3,2,0:T(8,128)S(1)}, ...), condition=%wide.region_5.6_spmd.clone, body=%wide.region_0.5_spmd.clone.sunk | while | flops 280316928 | bytes 10889621 | solution.py:100
  378.7 1.3 fusion.108
  380.1 1.6 fusion.110
  382.6 1.7 fusion.115
  384.4 1.3 fusion.108
  385.8 1.6 fusion.110
  388.3 1.8 fusion.115
  390.2 1.3 fusion.108
  391.5 1.6 fusion.110
  394.1 1.7 fusion.115
  395.8 1.3 fusion.108
  397.2 1.6 fusion.110
  399.7 1.7 fusion.115
  401.5 1.3 fusion.108
  402.9 1.6 fusion.110
  405.4 1.7 fusion.115
  407.2 1.3 fusion.108
  408.6 1.6 fusion.110
  411.1 1.7 fusion.115
  412.9 1.3 fusion.108
  414.3 1.6 fusion.110
  416.8 1.7 fusion.115
  418.7 1.3 fusion.108
  420.0 1.6 fusion.110
  422.6 1.7 fusion.115
  425.3 10.2 %all-to-all-start.1 = ((f32[64,1,256]{2,1,0:T(1,128)}), f32[64,1,256]{2,1,0:T(1,128)S(1)}, u32[]{:S(2)}, u32[]{:S(2)}) async-start(f32[64,1,256]{2,1,0:T(1,128)} %reshape.371), calls=%async_computation.1 | async-start | bytes 131072 | tf_op jit(solution)/shard_map/all_to_all | solution.py:115
  436.5 8.3 %all-to-all-done.1 = f32[64,1,256]{2,1,0:T(1,128)S(1)} async-done(((f32[64,1,256]{2,1,0:T(1,128)}), f32[64,1,256]{2,1,0:T(1,128)S(1)}, u32[]{:S(2)}, u32[]{:S(2)}) %all-to-all-start.1) | async-done | bytes 65568 | tf_op jit(solution)/shard_map/all_to_all | solution.py:115
  444.8 5.4 all-to-all-start.2
  450.3 9.0 %copy.113 = f32[8,256,1024]{2,0,1:T(8,128)} copy(f32[8,256,1024]{1,2,0:T(8,128)} %bitcast.271) | data formatting | bytes 16777216 | tf_op jit(solution)/shard_map/reshape | solution.py:105
  459.3 9.3 %reshape.334 = f32[4,64,16,512]{3,2,1,0:T(8,128)} reshape(f32[256,8,1024]{2,1,0:T(8,128)} %bitcast.267) | data formatting | bytes 16777216 | tf_op jit(solution)/shard_map/reshape | solution.py:106
  468.6 11.5 %copy.114 = f32[4,16,64,512]{3,2,1,0:T(8,128)} copy(f32[4,16,64,512]{3,1,2,0:T(8,128)} %bitcast.268) | data formatting | bytes 16777216 | tf_op jit(solution)/shard_map/transpose | solution.py:106
  480.1 11.0 %all-to-all-start = ((f32[64,64,512]{2,1,0:T(8,128)}), f32[64,64,512]{2,1,0:T(8,128)}, u32[]{:S(2)}, u32[]{:S(2)}) async-start(f32[64,64,512]{2,1,0:T(8,128)} %bitcast.266), calls=%async_computation | async-start | bytes 16777216 | tf_op jit(solution)/shard_map/all_to_all | solution.py:112
  491.2 1.8 fusion.81
  493.7 159.7 %all_gather.25 = bf16[16,2,4,1024]{3,2,1,0:T(4,128)(2,1)S(1)} all-gather(bf16[1,2,4,1024]{3,2,1,0:T(4,128)(2,1)S(1)} %copy-done), channel_id=1, replica_groups=mesh['sect'=4,'ctx'=4,'tp'=16] {'sect','ctx'}, dimensions={0}, use_global_device_ids=true | all-gather | bytes 278528 | tf_op jit(solution)/shard_map/all_gather | solution.py:142
  653.6 30.1 %all-gather = bf16[4,8192]{1,0:T(4,128)(2,1)S(1)} all-gather(bf16[4,512]{1,0:T(4,128)(2,1)S(1)} %copy-done.1), channel_id=2, replica_groups=mesh['sect'=4,'ctx'=4,'tp'=16] {'tp'}, dimensions={1}, use_global_device_ids=true | all-gather | bytes 69632 | tf_op jit(solution)/shard_map/all_gather | solution.py:140
  686.3 0.8 fusion.58
  687.1 20.9 %all-gather.1 = f32[64,8,8]{2,1,0:T(8,128)S(1)} all-gather(f32[4,8,8]{2,1,0:T(8,128)S(1)} %copy_maximum_fusion), channel_id=3, replica_groups=mesh['sect'=4,'ctx'=4,'tp'=16] {'tp'}, dimensions={0}, use_global_device_ids=true | all-gather | bytes 17408 | tf_op jit(solution)/shard_map/all_gather | solution.py:17
  708.2 24.5 %all-gather.2 = f32[64,8,8]{2,1,0:T(8,128)S(1)} all-gather(f32[4,8,8]{2,1,0:T(8,128)S(1)} %copy_add_fusion), channel_id=4, replica_groups=mesh['sect'=4,'ctx'=4,'tp'=16] {'tp'}, dimensions={0}, use_global_device_ids=true | all-gather | bytes 17408 | tf_op jit(solution)/shard_map/all_gather | solution.py:17
  732.7 2.6 all-gather.9.cloned.1.call-done
  735.3 0.9 slice.51
  736.3 16.9 %while.34 = (s32[]{:T(128)}, f32[4,8,8]{2,1,0:T(8,128)S(1)}, f32[4,8,8]{2,1,0:T(8,128)S(1)}, f32[4,8,8,128]{3,2,1,0:T(8,128)S(1)}, f32[16,4,8,8]{3,2,1,0:T(8,128...) while((s32[]{:T(128)}, f32[4,8,8]{2,1,0:T(8,128)S(1)}, ...), condition=%wide.region_15.16_spmd, body=%wide.region_14.15_spmd.sunk | while | flops 99845 | bytes 403607 | solution.py:23
  736.3 1.1 fusion.103
  737.4 1.1 fusion.103
  738.6 1.1 fusion.103
  739.7 1.1 fusion.103
  740.8 1.1 fusion.103
  741.9 1.1 fusion.103
  743.1 1.1 fusion.103
  744.2 1.1 fusion.103
  745.3 1.1 fusion.103
  746.5 1.1 fusion.103
  747.6 1.1 fusion.103
  748.7 1.1 fusion.103
  749.9 1.1 fusion.103
  751.0 1.1 fusion.103
  752.1 1.1 fusion.103
  755.4 0.8 reduce.6
  757.5 7.1 mul.182
  764.6 10.3 %mul.183 = f32[64,64,512]{2,1,0:T(8,128)} reshape(f32[64,64,4,128]{3,2,1,0:T(4,128)} %mul.182) | data formatting | bytes 16777216 | tf_op jit(solution)/shard_map/mul | solution.py:40
  774.9 7.6 multiply_reduce_fusion
  (130 shorter events, 19.9 us)
Async XLA Ops:
  8.0 358.4 %all-gather.7.cloned.1.call-start = ((), (), s32[]{:S(2)}) async-start(), calls=%async_computation.3 | async-start | bytes 4259840 | tf_op jit(solution)/shard_map/all_gather | solution.py:75
  8.8 2.4 copy-start
  425.3 19.5 %all-to-all-start.1 = ((f32[64,1,256]{2,1,0:T(1,128)}), f32[64,1,256]{2,1,0:T(1,128)S(1)}, u32[]{:S(2)}, u32[]{:S(2)}) async-start(f32[64,1,256]{2,1,0:T(1,128)} %reshape.371), calls=%async_computation.1 | async-start | bytes 131072 | tf_op jit(solution)/shard_map/all_to_all | solution.py:115
  444.8 35.2 %all-to-all-start.2 = ((f32[64,1,256]{2,1,0:T(1,128)}), f32[64,1,256]{2,1,0:T(1,128)S(1)}, u32[]{:S(2)}, u32[]{:S(2)}) async-start(f32[64,1,256]{2,1,0:T(1,128)} %reshape.369), calls=%async_computation.2 | async-start | bytes 131072 | tf_op jit(solution)/shard_map/all_to_all | solution.py:118
  480.1 294.8 %all-to-all-start = ((f32[64,64,512]{2,1,0:T(8,128)}), f32[64,64,512]{2,1,0:T(8,128)}, u32[]{:S(2)}, u32[]{:S(2)}) async-start(f32[64,64,512]{2,1,0:T(8,128)} %bitcast.266), calls=%async_computation | async-start | bytes 16777216 | tf_op jit(solution)/shard_map/all_to_all | solution.py:112
  491.1 244.2 %all-gather.9.cloned.1.call-start = ((), (), s32[]{:S(2)}) async-start(), calls=%async_computation.4 | async-start | bytes 2228224 | tf_op jit(solution)/shard_map/all_gather | solution.py:17
  493.0 160.6 %copy-start.1 = (bf16[4,512]{1,0:T(4,128)(2,1)S(1)}, bf16[4,512]{1,0:T(4,128)(2,1)}, u32[]{:S(2)}) copy-start(bf16[4,512]{1,0:T(4,128)(2,1)} %param.16) | copy-start | bytes 12292
  493.0 190.6 %copy-start.2 = (s32[4]{0:T(128)S(1)}, s32[4]{0:T(128)}, u32[]{:S(2)}) copy-start(s32[4]{0:T(128)} %param.19) | copy-start | bytes 52
  493.0 190.7 %copy-start.3 = (s32[4]{0:T(128)S(1)}, s32[4]{0:T(128)}, u32[]{:S(2)}) copy-start(s32[4]{0:T(128)} %param.18) | copy-start | bytes 52
Sparse Core Ops, SparseCore 0:
  10.6 355.7 all-gather.6
Sparse Core Ops, SparseCore 1:
  687.2 48.1 all-gather.8
where the time goes:
time: 793 us; the launch traced here: 791 us
  waiting for transfers between devices  367 us (46%)
  blocking collectives  235 us (30%)
  local copies, waits for them, and re-layouts  69.3 us (9%)
  matrix products  41.7 us (5%)
  other arithmetic  33.5 us (4%)
  starting transfers between devices  26.8 us (3%)
  between operations  16.5 us (2%)
    all_gather x1, waiting for transfers between devices, spread_positions(): gathered = lax.all_gather(span_queries, ('ctx', 'tp'), axis=0, tiled=True)  355 us
    all_gather x1, blocking collectives, decode_step(): arrived = lax.all_gather(span_kv, ('sect', 'ctx'), axis=0, tiled=True)  160 us
    all_gather x2, blocking collectives, merged(): everything = jax.tree.map(lambda part: lax.all_gather(part, axis), x)  45.3 us
    all_gather x1, blocking collectives, decode_step(): lax.all_gather(decode_queries[:, None, :], 'tp', axis=1, tiled=True)  30.1 us
    dot_general x16, matrix products, partial_block(): jnp.einsum('tkgd,pkd->tkgp', queries, key_rows, preferred_element_type=jn...  22.8 us
    mul x2, local copies, waits for them, and re-layouts, fold_parts(): combined = jnp.sum(sums * factor[..., None], axis=stack_dim)  17.4 us
    dot_general x16, matrix products, partial_block(): jnp.einsum('tkgp,pkd->tkgd', weights.astype(jnp.bfloat16), value_rows, pr...  16.7 us
    add x15, other arithmetic, join_pair(): former[2] * left_factor[..., None] + latter[2] * right_factor[..., None]  16.1 us
  transfers between devices with their start and end apart: 5, of which 3 were waited for; matrix products, arithmetic and copies ran while one was open for 10% of the time, Pallas kernels for 0%

commit v1 on v0

v1 whole, which is shorter than its diff:
```python
import math

import jax
import jax.numpy as jnp
from jax import lax
from jax.experimental import pallas as pl
from jax.experimental.pallas import tpu as pltpu
from jax.sharding import PartitionSpec as P

HEAD_DIM = 128
MESH = pl.DeviceIdType.MESH
NEG = -1e30
EXP2_SCALE = math.log2(math.e) / math.sqrt(HEAD_DIM)
F32 = jnp.float32
BF16 = jnp.bfloat16


def dot_nt(a, b):
    return lax.dot_general(a, b, (((1,), (1,)), ((), ())), preferred_element_type=F32)


def dot_nn(a, b):
    return lax.dot_general(a, b, (((1,), (0,)), ((), ())), preferred_element_type=F32)


def iota(shape, dim):
    return lax.broadcasted_iota(jnp.int32, shape, dim)


def select4(index, values):
    return jnp.where(
        index == 0,
        values[0],
        jnp.where(index == 1, values[1], jnp.where(index == 2, values[2], values[3])),
    )


def kernel(
    off_ref,
    len_ref,
    own_ref,
    dq_ref,
    skv_ref,
    q_hbm,
    pc_hbm,
    dc_hbm,
    out_ref,
    dout_ref,
    cache,
    kv,
    vt,
    q_all,
    scores,
    po_send,
    po_recv,
    ps_send,
    ps_recv,
    sp_head,
    sp_pre,
    sp_block,
    sp_all,
    sp_wide,
    dq_wide,
    dq_block,
    dq_all,
    dp_send,
    dp_recv,
    d_result,
    local_sem,
    kv_ssem,
    kv_rsem,
    q_ssem,
    q_rsem,
    sp_ssem,
    sp_rsem,
    sa_ssem,
    sa_rsem,
    dq_ssem,
    dq_rsem,
    dp_ssem,
    dp_rsem,
    po_ssem,
    po_rsem,
    ps_ssem,
    ps_rsem,
):
    s = lax.axis_index("sect")
    c = lax.axis_index("ctx")
    t = lax.axis_index("tp")
    y = t // 4
    x = t % 4
    head = t // 2
    pair = t + 1 - 2 * (t % 2)

    def kv_peer(slot, sign):
        a, b = slot // 2, slot % 2
        far_y = (y + sign * a + 4) % 4
        far_x = x + b * (3 - 2 * x)
        return far_y * 4 + far_x

    def q_peer(slot, sign):
        a, b = slot // 2, slot % 2
        return (c + sign * a + 4) % 4, t + b * (pair - t)

    def span_peer(step):
        g = (s * 4 + c + step) % 16
        return g // 4, g % 4

    def kv_copy(slot):
        far = kv_peer(slot, 1)
        column = pl.multiple_of((far // 2) * HEAD_DIM, HEAD_DIM)
        return pltpu.make_async_remote_copy(
            src_ref=pc_hbm.at[0, :, :, pl.ds(column, HEAD_DIM)],
            dst_ref=kv.at[slot],
            send_sem=kv_ssem.at[slot],
            recv_sem=kv_rsem.at[slot],
            device_id=(s, c, far),
            device_id_type=MESH,
        )

    def q_copy(slot):
        far_c, far_t = q_peer(slot, 1)
        return pltpu.make_async_remote_copy(
            src_ref=q_hbm.at[0],
            dst_ref=q_all.at[slot],
            send_sem=q_ssem.at[slot],
            recv_sem=q_rsem.at[slot],
            device_id=(s, far_c, far_t),
            device_id_type=MESH,
        )

    def sp_copy(slot):
        far = kv_peer(slot, 1)
        return pltpu.make_async_remote_copy(
            src_ref=sp_head.at[far // 2],
            dst_ref=sp_pre.at[slot],
            send_sem=sp_ssem.at[slot],
            recv_sem=sp_rsem.at[slot],
            device_id=(s, c, far),
            device_id_type=MESH,
        )

    def sa_copy(step):
        far_s, far_c = span_peer(step)
        return pltpu.make_async_remote_copy(
            src_ref=sp_block,
            dst_ref=sp_all.at[s * 4 + c],
            send_sem=sa_ssem.at[step],
            recv_sem=sa_rsem.at[step],
            device_id=(far_s, far_c, t),
            device_id_type=MESH,
        )

    def dq_copy(step):
        return pltpu.make_async_remote_copy(
            src_ref=dq_block,
            dst_ref=dq_all.at[t],
            send_sem=dq_ssem.at[step],
            recv_sem=dq_rsem.at[step],
            device_id=(s, c, (t + step) % 16),
            device_id_type=MESH,
        )

    def dp_copy(step):
        far = (t + step) % 16
        return pltpu.make_async_remote_copy(
            src_ref=dp_send.at[far],
            dst_ref=dp_recv.at[step],
            send_sem=dp_ssem.at[step],
            recv_sem=dp_rsem.at[step],
            device_id=(s, c, far),
            device_id_type=MESH,
        )

    def po_copy(slot):
        far_c, far_t = q_peer(slot, -1)
        return pltpu.make_async_remote_copy(
            src_ref=po_send.at[slot],
            dst_ref=po_recv.at[slot],
            send_sem=po_ssem.at[slot],
            recv_sem=po_rsem.at[slot],
            device_id=(s, far_c, far_t),
            device_id_type=MESH,
        )

    def ps_copy(slot):
        far_c, far_t = q_peer(slot, -1)
        return pltpu.make_async_remote_copy(
            src_ref=ps_send.at[slot],
            dst_ref=ps_recv.at[slot],
            send_sem=ps_ssem.at[slot],
            recv_sem=ps_rsem.at[slot],
            device_id=(s, far_c, far_t),
            device_id_type=MESH,
        )

    own_column = pl.multiple_of(head * HEAD_DIM, HEAD_DIM)
    local_kv = pltpu.make_async_copy(
        pc_hbm.at[0, :, :, pl.ds(own_column, HEAD_DIM)], kv.at[0], local_sem.at[0]
    )
    local_q = pltpu.make_async_copy(q_hbm.at[0], q_all.at[0], local_sem.at[1])
    local_cache = pltpu.make_async_copy(dc_hbm, cache, local_sem.at[2])
    local_kv.start()
    local_q.start()
    local_cache.start()

    barrier = pltpu.get_barrier_semaphore()

    def greet(far_s, far_c, far_t):
        pl.semaphore_signal(
            barrier, inc=1, device_id=(far_s, far_c, far_t), device_id_type=MESH
        )

    for step in range(1, 16):
        greet(s, c, (t + step) % 16)
        far_s, far_c = span_peer(step)
        greet(far_s, far_c, t)
    for step in range(1, 4):
        greet(s, (c + step) % 4, pair)

    own_q = dq_ref[...].astype(F32)
    span_k = skv_ref[0, 0].astype(F32)
    span_v = skv_ref[0, 1].astype(F32)
    for h in range(4):
        dq_wide[4 * h : 4 * h + 4, :] = own_q[:, h * HEAD_DIM : (h + 1) * HEAD_DIM]
    for h in range(8):
        sp_head[h, 0:4, :] = span_k[:, h * HEAD_DIM : (h + 1) * HEAD_DIM]
        sp_head[h, 4:8, :] = span_v[:, h * HEAD_DIM : (h + 1) * HEAD_DIM]
    dq_block[...] = dq_wide[...].astype(BF16)
    sp_block[...] = sp_head[...].reshape(64, HEAD_DIM).astype(BF16)

    pl.semaphore_wait(barrier, 33)

    for step in range(1, 16):
        dq_copy(step).start()
    for slot in range(1, 8):
        kv_copy(slot).start()
        q_copy(slot).start()
        sp_copy(slot).start()
    for step in range(1, 16):
        sa_copy(step).start()

    dq_all[t] = dq_block[...]
    sp_all[s * 4 + c] = sp_block[...]
    sp_pre[0] = sp_head[head]

    local_cache.wait()
    for step in range(1, 16):
        dq_copy(step).wait_recv()
    for step in range(1, 16):
        sa_copy(step).wait_recv()
    sp_wide[...] = sp_all[...].astype(F32)
    row_q = iota((32, 512), 0) % 4
    row_p = iota((32, 512), 1) // 128
    pos = t * 128 + iota((32, 512), 1) % 128
    length = select4(row_p, [len_ref[r] for r in range(4)])
    cache_live = (row_q == row_p) & (pos < length)
    new_col = iota((32, 128), 1)
    new_owner = select4(new_col // 32, [own_ref[r] for r in range(4)])
    new_row = (s * 4 + c) * 4 + iota((32, 128), 0) % 4
    new_live = (new_owner == new_row) & (new_col % 8 < 4)

    def decode_head(k, carry):
        column = pl.ds(pl.multiple_of(k * HEAD_DIM, HEAD_DIM), HEAD_DIM)
        queries = dq_all[pl.ds(2 * k, 2)].reshape(32, HEAD_DIM)
        fresh = (
            sp_wide[:, pl.ds(pl.multiple_of(8 * k, 8), 8), :].reshape(128, HEAD_DIM).astype(BF16)
        )
        part = jnp.concatenate(
            [dot_nt(queries, cache[r, 0, :, column]) for r in range(4)], axis=1
        )
        part = jnp.where(cache_live, part, NEG)
        fresh_part = jnp.where(new_live, dot_nt(queries, fresh), NEG)
        top = jnp.maximum(
            jnp.max(part, axis=1, keepdims=True), jnp.max(fresh_part, axis=1, keepdims=True)
        )
        part = jnp.exp2((part - top) * EXP2_SCALE)
        fresh_part = jnp.exp2((fresh_part - top) * EXP2_SCALE)
        fresh_part = jnp.where(new_live, fresh_part, 0.0)
        total = jnp.sum(part, axis=1, keepdims=True) + jnp.sum(fresh_part, axis=1, keepdims=True)
        rounded = part.astype(BF16)
        acc = dot_nn(pltpu.roll(fresh_part, 4, axis=1).astype(BF16), fresh)
        for r in range(4):
            acc += dot_nn(rounded[:, r * 128 : (r + 1) * 128], cache[r, 1, :, column])
        stats = jnp.where(iota((32, 128), 1) < 64, top, total)
        dp_send[pl.ds(2 * k, 2), 0] = acc.reshape(2, 16, HEAD_DIM)
        dp_send[pl.ds(2 * k, 2), 1] = stats.reshape(2, 16, HEAD_DIM)
        return carry

    lax.fori_loop(0, 8, decode_head, 0)
    for step in range(1, 16):
        dp_copy(step).start()

    local_kv.wait()
    local_q.wait()
    for slot in range(1, 8):
        sp_copy(slot).wait_recv()
    for slot in range(1, 8):
        kv_copy(slot).wait_recv()
    for slot in range(8):
        vt[:, slot * 256 : (slot + 1) * 256] = kv[slot, 1].astype(F32).T.astype(BF16)
    span_rows = sp_pre[...].reshape(64, HEAD_DIM)
    span_keys = span_rows.astype(BF16)
    span_vt = pltpu.roll(span_rows, 60, axis=0).T.astype(BF16)
    offset = off_ref[0]
    span_row = iota((64, 256), 0)
    span_slot = span_row // 8
    span_y = (y - span_slot // 2 + 4) % 4
    span_x = x + (span_slot % 2) * (3 - 2 * x)
    span_token = (c * 16 + span_y * 4 + span_x) * 4 + span_row % 8
    span_real = span_row % 8 < 4

    def chunk(i, carry):
        slot = 7 - i
        far_c, _ = q_peer(slot, -1)

        @pl.when(slot > 0)
        def _():
            q_copy(slot).wait_recv()

        block = q_all[slot]
        queries = jnp.concatenate(
            [block[:, h * HEAD_DIM : (h + 1) * HEAD_DIM] for h in range(4)], axis=0
        )
        span_live = span_real & (span_token <= far_c * 64 + iota((64, 256), 1) % 64)
        span_part = jnp.where(span_live, dot_nt(span_keys, queries), NEG)
        top = jnp.max(span_part.reshape(8, 8, 256), axis=0)
        for b in range(8):
            start = (c * 16 + kv_peer(b, -1)) * 256
            part = dot_nt(kv[b, 0], queries)
            part = jnp.where(start + iota((256, 256), 0) < offset, part, NEG)
            scores[b] = part
            top = jnp.maximum(top, jnp.max(part.reshape(32, 8, 256), axis=0))
        top = jnp.max(top, axis=0, keepdims=True)
        weights = jnp.where(span_live, jnp.exp2((span_part - top) * EXP2_SCALE), 0.0)
        total = jnp.sum(weights.reshape(8, 8, 256), axis=0)
        acc = dot_nn(span_vt, weights.astype(BF16))
        for b in range(8):
            weights = jnp.exp2((scores[b] - top) * EXP2_SCALE)
            total += jnp.sum(weights.reshape(32, 8, 256), axis=0)
            acc += dot_nn(vt[:, b * 256 : (b + 1) * 256], weights.astype(BF16))
        total = jnp.sum(total, axis=0, keepdims=True)
        po_send[slot] = acc.astype(BF16)
        ps_send[slot] = jnp.where(iota((8, 256), 0) < 4, top, total)

        @pl.when(slot > 0)
        def _():
            po_copy(slot).start()
            ps_copy(slot).start()

        return carry

    lax.fori_loop(0, 8, chunk, 0)

    for step in range(1, 16):
        dp_copy(step).wait_recv()
    dp_recv[0] = dp_send[t]
    tops = [dp_recv[i, 1][:, 0:1] for i in range(16)]
    top = tops[0]
    for i in range(1, 16):
        top = jnp.maximum(top, tops[i])
    acc = jnp.zeros((16, HEAD_DIM), F32)
    total = jnp.zeros((16, 1), F32)
    for i in range(16):
        factor = jnp.exp2((tops[i] - top) * EXP2_SCALE)
        acc += dp_recv[i, 0] * factor
        total += dp_recv[i, 1][:, 64:65] * factor
    d_result[...] = acc / total
    for h in range(4):
        dout_ref[:, h * HEAD_DIM : (h + 1) * HEAD_DIM] = d_result[4 * h : 4 * h + 4, :].astype(BF16)

    for slot in range(1, 8):
        ps_copy(slot).wait_recv()
        po_copy(slot).wait_recv()
    ps_recv[0] = ps_send[0]
    po_recv[0] = po_send[0]
    top = ps_recv[0, 0:1, :]
    for i in range(1, 8):
        top = jnp.maximum(top, ps_recv[i, 0:1, :])
    acc = jnp.zeros((HEAD_DIM, 256), F32)
    total = jnp.zeros((1, 256), F32)
    for i in range(8):
        factor = jnp.exp2((ps_recv[i, 0:1, :] - top) * EXP2_SCALE)
        acc += po_recv[i].astype(F32) * factor
        total += ps_recv[i, 4:5, :] * factor
    result = (acc / total).T
    for h in range(4):
        out_ref[0, :, h * HEAD_DIM : (h + 1) * HEAD_DIM] = result[h * 64 : (h + 1) * 64].astype(BF16)

    for step in range(1, 16):
        dq_copy(step).wait_send()
        sa_copy(step).wait_send()
        dp_copy(step).wait_send()
    for slot in range(1, 8):
        kv_copy(slot).wait_send()
        q_copy(slot).wait_send()
        sp_copy(slot).wait_send()
        po_copy(slot).wait_send()
        ps_copy(slot).wait_send()


def body(
    span_queries,
    prompt_cache,
    span_kv,
    span_offsets,
    decode_queries,
    decode_cache,
    cache_lengths,
    owner_rows,
):
    smem = pl.BlockSpec(memory_space=pltpu.SMEM)
    vmem = pl.BlockSpec(memory_space=pltpu.VMEM)
    hbm = pl.BlockSpec(memory_space=pl.ANY)
    sem = pltpu.SemaphoreType.DMA
    return pl.pallas_call(
        kernel,
        out_shape=(
            jax.ShapeDtypeStruct(span_queries.shape, BF16),
            jax.ShapeDtypeStruct(decode_queries.shape, BF16),
        ),
        in_specs=[smem, smem, smem, vmem, vmem, hbm, hbm, hbm],
        out_specs=(vmem, vmem),
        scratch_shapes=[
            pltpu.VMEM((4, 2, 128, 1024), BF16),
            pltpu.VMEM((8, 2, 256, HEAD_DIM), BF16),
            pltpu.VMEM((HEAD_DIM, 2048), BF16),
            pltpu.VMEM((8, 64, 512), BF16),
            pltpu.VMEM((8, 256, 256), F32),
            pltpu.VMEM((8, HEAD_DIM, 256), BF16),
            pltpu.VMEM((8, HEAD_DIM, 256), BF16),
            pltpu.VMEM((8, 8, 256), F32),
            pltpu.VMEM((8, 8, 256), F32),
            pltpu.VMEM((8, 8, HEAD_DIM), F32),
            pltpu.VMEM((8, 8, HEAD_DIM), F32),
            pltpu.VMEM((64, HEAD_DIM), BF16),
            pltpu.VMEM((16, 64, HEAD_DIM), BF16),
            pltpu.VMEM((16, 64, HEAD_DIM), F32),
            pltpu.VMEM((16, HEAD_DIM), F32),
            pltpu.VMEM((16, HEAD_DIM), BF16),
            pltpu.VMEM((16, 16, HEAD_DIM), BF16),
            pltpu.VMEM((16, 2, 16, HEAD_DIM), F32),
            pltpu.VMEM((16, 2, 16, HEAD_DIM), F32),
            pltpu.VMEM((16, HEAD_DIM), F32),
            sem((3,)),
            sem((8,)),
            sem((8,)),
            sem((8,)),
            sem((8,)),
            sem((8,)),
            sem((8,)),
            sem((16,)),
            sem((16,)),
            sem((16,)),
            sem((16,)),
            sem((16,)),
            sem((16,)),
            sem((8,)),
            sem((8,)),
            sem((8,)),
            sem((8,)),
        ],
        compiler_params=pltpu.CompilerParams(
            collective_id=0, has_side_effects=True, vmem_limit_bytes=48 * 1024 * 1024
        ),
    )(
        span_offsets,
        cache_lengths,
        owner_rows,
        decode_queries,
        span_kv,
        span_queries,
        prompt_cache,
        decode_cache,
    )


def solution(mesh):
    return jax.shard_map(
        body,
        mesh=mesh,
        in_specs=(
            P("sect", "ctx", "tp"),
            P("sect", None, ("ctx", "tp"), None),
            P("sect", None, ("ctx", "tp"), None),
            P("sect"),
            P(("sect", "ctx"), "tp"),
            P(("sect", "ctx"), None, "tp", None),
            P(("sect", "ctx")),
            P(),
        ),
        out_specs=(P("sect", "ctx", "tp"), P(("sect", "ctx"), "tp")),
        check_vma=False,
    )
```

time: 793 us -> 60.6 us (0.08)
  the two profiles are of different devices: /device:TPU:2 before, /device:TPU:39 now
where the time goes in v1:
time: 60.6 us; the launch traced here: 60.3 us
  Pallas kernels  51.4 us (85%)
  local copies, waits for them, and re-layouts  7.58 us (13%)
  between operations  1.3 us (2%)
    pallas_call x1, Pallas kernels, body(): pl.pallas_call(kernel, out_shape=(jax.ShapeDtypeStruct(span_queries.shape...  51.4 us
    unnamed x16, local copies, waits for them, and re-layouts  7.58 us

profile of v1, /device:TPU:39, one launch (start us, length us, event | category | flops | bytes accessed | tf_op | source)
XLA Modules:
  0.0 60.3 jit_solution(8655906734913687367)
XLA Ops:
  1.3 0.0 copy-start
  1.3 1.6 %copy-done = bf16[4,2,128,1024]{3,2,1,0:T(8,128)(2,1)S(1)} copy-done((bf16[4,2,128,1024]{3,2,1,0:T(8,128)(2,1)S(1)}, bf16[4,2,128,1024]{3,2,1,0:T(8,128)(2,1)}, u32[]{:S(2)}) %copy-start) | copy-done | bytes 2097176
  2.9 0.0 copy-start.1
  2.9 1.2 %copy-done.1 = bf16[1,2,256,1024]{3,2,1,0:T(8,128)(2,1)S(1)} copy-done((bf16[1,2,256,1024]{3,2,1,0:T(8,128)(2,1)S(1)}, bf16[1,2,256,1024]{3,2,1,0:T(8,128)(2,1)}, u32[]{:S(2)}) %copy-start.1) | copy-done | bytes 1048600
  4.1 0.0 copy-start.2
  4.1 0.8 %copy-done.2 = bf16[1,64,512]{2,1,0:T(8,128)(2,1)S(1)} copy-done((bf16[1,64,512]{2,1,0:T(8,128)(2,1)S(1)}, bf16[1,64,512]{2,1,0:T(8,128)(2,1)}, u32[]{:S(2)}) %copy-start.2) | copy-done | bytes 65560
  4.9 0.0 copy-start.3
  4.9 0.7 %copy-done.3 = bf16[1,2,4,1024]{3,2,1,0:T(4,128)(2,1)S(1)} copy-done((bf16[1,2,4,1024]{3,2,1,0:T(4,128)(2,1)S(1)}, bf16[1,2,4,1024]{3,2,1,0:T(4,128)(2,1)}, u32[]{:S(2)}) %copy-start.3) | copy-done | bytes 16408
  5.7 0.0 copy-start.4
  5.7 0.7 %copy-done.4 = bf16[4,512]{1,0:T(4,128)(2,1)S(1)} copy-done((bf16[4,512]{1,0:T(4,128)(2,1)S(1)}, bf16[4,512]{1,0:T(4,128)(2,1)}, u32[]{:S(2)}) %copy-start.4) | copy-done | bytes 4120
  6.3 0.0 copy-start.5
  6.3 0.7 %copy-done.5 = s32[4]{0:T(128)S(1)} copy-done((s32[4]{0:T(128)S(1)}, s32[4]{0:T(128)}, u32[]{:S(2)}) %copy-start.5) | copy-done | bytes 40
  7.0 0.0 copy-start.6
  7.0 0.7 %copy-done.6 = s32[4]{0:T(128)S(1)} copy-done((s32[4]{0:T(128)S(1)}, s32[4]{0:T(128)}, u32[]{:S(2)}) %copy-start.6) | copy-done | bytes 40
  7.7 51.4 %shard_map.95 = (bf16[1,64,512]{2,1,0:T(8,128)(2,1)S(1)}, bf16[4,512]{1,0:T(4,128)(2,1)S(1)}) custom-call(s32[1]{0:T(128)S(6)} %copy.12.off_ref, s32[4]{0:T(128)S(1)} %copy-done.5, s32[4]{0:T(128)S(1)} %copy-done.6, bf16[4,512]{1,0:T(4,128)(2,1)S(1)} %copy-done.4, bf16[1,2,4,1024]{3,2,1,0:T(4,128)(2,1)S(1)} %copy-done.3, bf16[1,64,512]{2,1,0:T(8,128)(2,1)S(1)} %copy-done.2, ...), custom_call_target="tpu_custom_call" | custom-call | tf_op jit(solution)/shard_map/pallas_call | solution.py:416
  59.0 0.6 %copy.13 = bf16[1,64,512]{2,1,0:T(8,128)(2,1)} copy(bf16[1,64,512]{2,1,0:T(8,128)(2,1)S(1)} %get-tuple-element.4) | data formatting | bytes 131072
  59.7 0.6 copy.14
Async XLA Ops:
  1.3 1.6 %copy-start = (bf16[4,2,128,1024]{3,2,1,0:T(8,128)(2,1)S(1)}, bf16[4,2,128,1024]{3,2,1,0:T(8,128)(2,1)}, u32[]{:S(2)}) copy-start(bf16[4,2,128,1024]{3,2,1,0:T(8,128)(2,1)} %dc_hbm.1) | copy-start | bytes 6291460
  2.9 1.2 %copy-start.1 = (bf16[1,2,256,1024]{3,2,1,0:T(8,128)(2,1)S(1)}, bf16[1,2,256,1024]{3,2,1,0:T(8,128)(2,1)}, u32[]{:S(2)}) copy-start(bf16[1,2,256,1024]{3,2,1,0:T(8,128)(2,1)} %pc_hbm.1) | copy-start | bytes 3145732
  4.1 0.8 %copy-start.2 = (bf16[1,64,512]{2,1,0:T(8,128)(2,1)S(1)}, bf16[1,64,512]{2,1,0:T(8,128)(2,1)}, u32[]{:S(2)}) copy-start(bf16[1,64,512]{2,1,0:T(8,128)(2,1)} %q_hbm.1) | copy-start | bytes 196612
  4.9 0.7 %copy-start.3 = (bf16[1,2,4,1024]{3,2,1,0:T(4,128)(2,1)S(1)}, bf16[1,2,4,1024]{3,2,1,0:T(4,128)(2,1)}, u32[]{:S(2)}) copy-start(bf16[1,2,4,1024]{3,2,1,0:T(4,128)(2,1)} %skv_ref.1) | copy-start | bytes 49156
  5.7 0.7 %copy-start.4 = (bf16[4,512]{1,0:T(4,128)(2,1)S(1)}, bf16[4,512]{1,0:T(4,128)(2,1)}, u32[]{:S(2)}) copy-start(bf16[4,512]{1,0:T(4,128)(2,1)} %dq_ref.1) | copy-start | bytes 12292
  6.3 0.7 %copy-start.5 = (s32[4]{0:T(128)S(1)}, s32[4]{0:T(128)}, u32[]{:S(2)}) copy-start(s32[4]{0:T(128)} %len_ref.1) | copy-start | bytes 52
  7.0 0.7 %copy-start.6 = (s32[4]{0:T(128)S(1)}, s32[4]{0:T(128)}, u32[]{:S(2)}) copy-start(s32[4]{0:T(128)} %own_ref.1) | copy-start | bytes 52

commit v2 on v1

--- a/solution.py
+++ b/solution.py
@@ -13,6 +13,8 @@
 EXP2_SCALE = math.log2(math.e) / math.sqrt(HEAD_DIM)
 F32 = jnp.float32
 BF16 = jnp.bfloat16
+NEAR = (0, 1, 2, 6, 3, 7)
+FAR = (4, 5)
 
 
 def dot_nt(a, b):
@@ -36,21 +38,29 @@
 
 
 def kernel(
+    off_hbm,
+    len_hbm,
+    own_hbm,
+    dq_hbm,
+    skv_hbm,
+    q_hbm,
+    pc_hbm,
+    dc_hbm,
+    out_ref,
+    dout_ref,
     off_ref,
     len_ref,
     own_ref,
     dq_ref,
     skv_ref,
-    q_hbm,
-    pc_hbm,
-    dc_hbm,
-    out_ref,
-    dout_ref,
     cache,
     kv,
     vt,
     q_all,
     scores,
+    run_top,
+    run_total,
+    run_acc,
     po_send,
     po_recv,
     ps_send,
@@ -102,9 +112,12 @@
         a, b = slot // 2, slot % 2
         return (c + sign * a + 4) % 4, t + b * (pair - t)
 
+    core = s % 2
+    layer = (s // 2) * 4 + c
+
     def span_peer(step):
-        g = (s * 4 + c + step) % 16
-        return g // 4, g % 4
+        far = (layer + step) % 8
+        return (far // 4) * 2 + core, far % 4
 
     def kv_copy(slot):
         far = kv_peer(slot, 1)
@@ -118,14 +131,23 @@
             device_id_type=MESH,
         )
 
-    def q_copy(slot):
-        far_c, far_t = q_peer(slot, 1)
+    def q_copy(step):
         return pltpu.make_async_remote_copy(
             src_ref=q_hbm.at[0],
-            dst_ref=q_all.at[slot],
-            send_sem=q_ssem.at[slot],
-            recv_sem=q_rsem.at[slot],
-            device_id=(s, far_c, far_t),
+            dst_ref=q_all.at[2 * step],
+            send_sem=q_ssem.at[2 * step],
+            recv_sem=q_rsem.at[2 * step],
+            device_id=(s, (c + step) % 4, t),
+            device_id_type=MESH,
+        )
+
+    def q_forward(step):
+        return pltpu.make_async_remote_copy(
+            src_ref=q_all.at[2 * step],
+            dst_ref=q_all.at[2 * step + 1],
+            send_sem=q_ssem.at[2 * step + 1],
+            recv_sem=q_rsem.at[2 * step + 1],
+            device_id=(s, c, pair),
             device_id_type=MESH,
         )
 
@@ -144,10 +166,20 @@
         far_s, far_c = span_peer(step)
         return pltpu.make_async_remote_copy(
             src_ref=sp_block,
-            dst_ref=sp_all.at[s * 4 + c],
+            dst_ref=sp_all.at[s // 2, core, c],
             send_sem=sa_ssem.at[step],
             recv_sem=sa_rsem.at[step],
             device_id=(far_s, far_c, t),
+            device_id_type=MESH,
+        )
+
+    def sa_forward():
+        return pltpu.make_async_remote_copy(
+            src_ref=sp_all.at[:, core],
+            dst_ref=sp_all.at[:, core],
+            send_sem=sa_ssem.at[0],
+            recv_sem=sa_rsem.at[0],
+            device_id=(s + 1 - 2 * core, c, t),
             device_id_type=MESH,
         )
 
@@ -194,30 +226,48 @@
             device_id_type=MESH,
         )
 
+    barrier = pltpu.get_barrier_semaphore()
+
+    def greet(far_s, far_c, far_t):
+        pl.semaphore_signal(
+            barrier, inc=1, device_id=(far_s, far_c, far_t), device_id_type=MESH
+        )
+
+    for step in range(1, 8):
+        far_s, far_c = span_peer(step)
+        greet(far_s, far_c, t)
+    for step in range(1, 16):
+        greet(s, c, (t + step) % 16)
+    for step in range(1, 4):
+        greet(s, (c + step) % 4, pair)
+    greet(s + 1 - 2 * core, c, t)
+
     own_column = pl.multiple_of(head * HEAD_DIM, HEAD_DIM)
+    local_small = [
+        pltpu.make_async_copy(source, target, local_sem.at[3 + i])
+        for i, (source, target) in enumerate(
+            [
+                (dq_hbm, dq_ref),
+                (skv_hbm, skv_ref),
+                (off_hbm, off_ref),
+                (len_hbm, len_ref),
+                (own_hbm, own_ref),
+            ]
+        )
+    ]
+    for copy in local_small:
+        copy.start()
     local_kv = pltpu.make_async_copy(
         pc_hbm.at[0, :, :, pl.ds(own_column, HEAD_DIM)], kv.at[0], local_sem.at[0]
     )
     local_q = pltpu.make_async_copy(q_hbm.at[0], q_all.at[0], local_sem.at[1])
     local_cache = pltpu.make_async_copy(dc_hbm, cache, local_sem.at[2])
+    local_q.start()
     local_kv.start()
-    local_q.start()
     local_cache.start()
 
-    barrier = pltpu.get_barrier_semaphore()
-
-    def greet(far_s, far_c, far_t):
-        pl.semaphore_signal(
-            barrier, inc=1, device_id=(far_s, far_c, far_t), device_id_type=MESH
-        )
-
-    for step in range(1, 16):
-        greet(s, c, (t + step) % 16)
-        far_s, far_c = span_peer(step)
-        greet(far_s, far_c, t)
-    for step in range(1, 4):
-        greet(s, (c + step) % 4, pair)
-
+    for copy in local_small:
+        copy.wait()
     own_q = dq_ref[...].astype(F32)
     span_k = skv_ref[0, 0].astype(F32)
     span_v = skv_ref[0, 1].astype(F32)
@@ -228,81 +278,121 @@
         sp_head[h, 4:8, :] = span_v[:, h * HEAD_DIM : (h + 1) * HEAD_DIM]
     dq_block[...] = dq_wide[...].astype(BF16)
     sp_block[...] = sp_head[...].reshape(64, HEAD_DIM).astype(BF16)
-
-    pl.semaphore_wait(barrier, 33)
+    dq_all[t] = dq_block[...]
+    sp_all[s // 2, core, c] = sp_block[...]
+    sp_pre[0] = sp_head[head]
+    local_q.wait()
+
+    pl.semaphore_wait(barrier, 26)
 
     for step in range(1, 16):
         dq_copy(step).start()
+    for slot in NEAR[1:]:
+        kv_copy(slot).start()
+    q_forward(0).start()
+    for step in range(1, 4):
+        q_copy(step).start()
+    for slot in FAR:
+        kv_copy(slot).start()
     for slot in range(1, 8):
-        kv_copy(slot).start()
-        q_copy(slot).start()
         sp_copy(slot).start()
-    for step in range(1, 16):
-        sa_copy(step).start()
-
-    dq_all[t] = dq_block[...]
-    sp_all[s * 4 + c] = sp_block[...]
-    sp_pre[0] = sp_head[head]
 
     local_cache.wait()
     for step in range(1, 16):
         dq_copy(step).wait_recv()
-    for step in range(1, 16):
-        sa_copy(step).wait_recv()
-    sp_wide[...] = sp_all[...].astype(F32)
     row_q = iota((32, 512), 0) % 4
     row_p = iota((32, 512), 1) // 128
     pos = t * 128 + iota((32, 512), 1) % 128
     length = select4(row_p, [len_ref[r] for r in range(4)])
     cache_live = (row_q == row_p) & (pos < length)
-    new_col = iota((32, 128), 1)
-    new_owner = select4(new_col // 32, [own_ref[r] for r in range(4)])
-    new_row = (s * 4 + c) * 4 + iota((32, 128), 0) % 4
-    new_live = (new_owner == new_row) & (new_col % 8 < 4)
-
-    def decode_head(k, carry):
+    left = iota((32, 128), 1) < 64
+
+    def decode_cached(k, carry):
         column = pl.ds(pl.multiple_of(k * HEAD_DIM, HEAD_DIM), HEAD_DIM)
         queries = dq_all[pl.ds(2 * k, 2)].reshape(32, HEAD_DIM)
-        fresh = (
-            sp_wide[:, pl.ds(pl.multiple_of(8 * k, 8), 8), :].reshape(128, HEAD_DIM).astype(BF16)
-        )
         part = jnp.concatenate(
             [dot_nt(queries, cache[r, 0, :, column]) for r in range(4)], axis=1
         )
         part = jnp.where(cache_live, part, NEG)
-        fresh_part = jnp.where(new_live, dot_nt(queries, fresh), NEG)
-        top = jnp.maximum(
-            jnp.max(part, axis=1, keepdims=True), jnp.max(fresh_part, axis=1, keepdims=True)
-        )
+        top = jnp.max(part, axis=1, keepdims=True)
         part = jnp.exp2((part - top) * EXP2_SCALE)
-        fresh_part = jnp.exp2((fresh_part - top) * EXP2_SCALE)
-        fresh_part = jnp.where(new_live, fresh_part, 0.0)
-        total = jnp.sum(part, axis=1, keepdims=True) + jnp.sum(fresh_part, axis=1, keepdims=True)
+        total = jnp.sum(part, axis=1, keepdims=True)
         rounded = part.astype(BF16)
-        acc = dot_nn(pltpu.roll(fresh_part, 4, axis=1).astype(BF16), fresh)
+        acc = jnp.zeros((32, HEAD_DIM), F32)
         for r in range(4):
             acc += dot_nn(rounded[:, r * 128 : (r + 1) * 128], cache[r, 1, :, column])
-        stats = jnp.where(iota((32, 128), 1) < 64, top, total)
         dp_send[pl.ds(2 * k, 2), 0] = acc.reshape(2, 16, HEAD_DIM)
-        dp_send[pl.ds(2 * k, 2), 1] = stats.reshape(2, 16, HEAD_DIM)
+        dp_send[pl.ds(2 * k, 2), 1] = jnp.where(left, top, total).reshape(2, 16, HEAD_DIM)
         return carry
 
-    lax.fori_loop(0, 8, decode_head, 0)
-    for step in range(1, 16):
-        dp_copy(step).start()
+    lax.fori_loop(0, 4, decode_cached, 0)
+    for step in (1, 3, 2):
+        q_copy(step).wait_recv()
+        q_forward(step).start()
+    for step in range(1, 8):
+        sa_copy(step).start()
+    lax.fori_loop(4, 8, decode_cached, 0)
 
     local_kv.wait()
-    local_q.wait()
+    offset = off_ref[0]
+
+    def load_queries(slot):
+        block = q_all[slot]
+        return jnp.concatenate(
+            [block[:, h * HEAD_DIM : (h + 1) * HEAD_DIM] for h in range(4)], axis=0
+        )
+
+    def attend(slots, queries, top):
+        for b in slots:
+            start = (c * 16 + kv_peer(b, -1)) * 256
+            part = dot_nt(kv[b, 0], queries)
+            part = jnp.where(start + iota((256, 256), 0) < offset, part, NEG)
+            scores[b] = part
+            top = jnp.maximum(top, jnp.max(part.reshape(32, 8, 256), axis=0))
+        return jnp.max(top, axis=0, keepdims=True)
+
+    def collect(slots, top, total, acc):
+        for b in slots:
+            weights = jnp.exp2((scores[b] - top) * EXP2_SCALE)
+            total += jnp.sum(weights.reshape(32, 8, 256), axis=0)
+            acc += dot_nn(vt[:, b * 256 : (b + 1) * 256], weights.astype(BF16))
+        return total, acc
+
+    def transpose_values(slots):
+        for slot in slots:
+            vt[:, slot * 256 : (slot + 1) * 256] = kv[slot, 1].astype(F32).T.astype(BF16)
+
+    for slot in NEAR[1:]:
+        kv_copy(slot).wait_recv()
+    transpose_values(NEAR)
+
+    def first_pass(i, carry):
+        slot = (i + 1) % 8
+
+        @pl.when(slot % 2 == 1)
+        def _():
+            q_forward(slot // 2).wait_recv()
+
+        queries = load_queries(slot)
+        top = attend(NEAR, queries, jnp.full((8, 256), NEG, F32))
+        total, acc = collect(
+            NEAR, top, jnp.zeros((8, 256), F32), jnp.zeros((HEAD_DIM, 256), F32)
+        )
+        run_top[slot] = jnp.broadcast_to(top, (8, 256))
+        run_total[slot] = total
+        run_acc[slot] = acc
+        return carry
+
+    lax.fori_loop(0, 8, first_pass, 0)
+
     for slot in range(1, 8):
         sp_copy(slot).wait_recv()
-    for slot in range(1, 8):
+    for slot in FAR:
         kv_copy(slot).wait_recv()
-    for slot in range(8):
-        vt[:, slot * 256 : (slot + 1) * 256] = kv[slot, 1].astype(F32).T.astype(BF16)
+    transpose_values(FAR)
     span_rows = sp_pre[...].reshape(64, HEAD_DIM)
     span_keys = span_rows.astype(BF16)
     span_vt = pltpu.roll(span_rows, 60, axis=0).T.astype(BF16)
-    offset = off_ref[0]
     span_row = iota((64, 256), 0)
     span_slot = span_row // 8
     span_y = (y - span_slot // 2 + 4) % 4
@@ -310,35 +400,19 @@
     span_token = (c * 16 + span_y * 4 + span_x) * 4 + span_row % 8
     span_real = span_row % 8 < 4
 
-    def chunk(i, carry):
-        slot = 7 - i
+    def second_pass(i, carry):
+        slot = (i + 1) % 8
         far_c, _ = q_peer(slot, -1)
-
-        @pl.when(slot > 0)
-        def _():
-            q_copy(slot).wait_recv()
-
-        block = q_all[slot]
-        queries = jnp.concatenate(
-            [block[:, h * HEAD_DIM : (h + 1) * HEAD_DIM] for h in range(4)], axis=0
-        )
+        queries = load_queries(slot)
         span_live = span_real & (span_token <= far_c * 64 + iota((64, 256), 1) % 64)
         span_part = jnp.where(span_live, dot_nt(span_keys, queries), NEG)
         top = jnp.max(span_part.reshape(8, 8, 256), axis=0)
-        for b in range(8):
-            start = (c * 16 + kv_peer(b, -1)) * 256
-            part = dot_nt(kv[b, 0], queries)
-            part = jnp.where(start + iota((256, 256), 0) < offset, part, NEG)
-            scores[b] = part
-            top = jnp.maximum(top, jnp.max(part.reshape(32, 8, 256), axis=0))
-        top = jnp.max(top, axis=0, keepdims=True)
+        top = attend(FAR, queries, jnp.maximum(top, run_top[slot]))
+        factor = jnp.exp2((run_top[slot] - top) * EXP2_SCALE)
         weights = jnp.where(span_live, jnp.exp2((span_part - top) * EXP2_SCALE), 0.0)
-        total = jnp.sum(weights.reshape(8, 8, 256), axis=0)
-        acc = dot_nn(span_vt, weights.astype(BF16))
-        for b in range(8):
-            weights = jnp.exp2((scores[b] - top) * EXP2_SCALE)
-            total += jnp.sum(weights.reshape(32, 8, 256), axis=0)
-            acc += dot_nn(vt[:, b * 256 : (b + 1) * 256], weights.astype(BF16))
+        total = run_total[slot] * factor + jnp.sum(weights.reshape(8, 8, 256), axis=0)
+        acc = run_acc[slot] * factor[0:1] + dot_nn(span_vt, weights.astype(BF16))
+        total, acc = collect(FAR, top, total, acc)
         total = jnp.sum(total, axis=0, keepdims=True)
         po_send[slot] = acc.astype(BF16)
         ps_send[slot] = jnp.where(iota((8, 256), 0) < 4, top, total)
@@ -350,7 +424,39 @@
 
         return carry
 
-    lax.fori_loop(0, 8, chunk, 0)
+    lax.fori_loop(0, 8, second_pass, 0)
+
+    for step in range(1, 8):
+        sa_copy(step).wait_recv()
+    sa_forward().start()
+    sa_forward().wait_recv()
+    sp_wide[...] = sp_all[...].reshape(16, 64, HEAD_DIM).astype(F32)
+    new_col = iota((32, 128), 1)
+    new_owner = select4(new_col // 32, [own_ref[r] for r in range(4)])
+    new_row = (s * 4 + c) * 4 + iota((32, 128), 0) % 4
+    new_live = (new_owner == new_row) & (new_col % 8 < 4)
+
+    def decode_fresh(k, carry):
+        queries = dq_all[pl.ds(2 * k, 2)].reshape(32, HEAD_DIM)
+        fresh = (
+            sp_wide[:, pl.ds(pl.multiple_of(8 * k, 8), 8), :].reshape(128, HEAD_DIM).astype(BF16)
+        )
+        stats = dp_send[pl.ds(2 * k, 2), 1].reshape(32, HEAD_DIM)
+        former = stats[:, 0:1]
+        part = jnp.where(new_live, dot_nt(queries, fresh), NEG)
+        top = jnp.maximum(former, jnp.max(part, axis=1, keepdims=True))
+        factor = jnp.exp2((former - top) * EXP2_SCALE)
+        part = jnp.where(new_live, jnp.exp2((part - top) * EXP2_SCALE), 0.0)
+        total = stats[:, 64:65] * factor + jnp.sum(part, axis=1, keepdims=True)
+        acc = dp_send[pl.ds(2 * k, 2), 0].reshape(32, HEAD_DIM) * factor
+        acc += dot_nn(pltpu.roll(part, 4, axis=1).astype(BF16), fresh)
+        dp_send[pl.ds(2 * k, 2), 0] = acc.reshape(2, 16, HEAD_DIM)
+        dp_send[pl.ds(2 * k, 2), 1] = jnp.where(left, top, total).reshape(2, 16, HEAD_DIM)
+        return carry
+
+    lax.fori_loop(0, 8, decode_fresh, 0)
+    for step in range(1, 16):
+        dp_copy(step).start()
 
     for step in range(1, 16):
         dp_copy(step).wait_recv()
@@ -389,11 +495,16 @@
 
     for step in range(1, 16):
         dq_copy(step).wait_send()
+        dp_copy(step).wait_send()
+    for step in range(4):
+        q_forward(step).wait_send()
+    for step in range(1, 4):
+        q_copy(step).wait_send()
+    for step in range(1, 8):
         sa_copy(step).wait_send()
-        dp_copy(step).wait_send()
+    sa_forward().wait_send()
     for slot in range(1, 8):
         kv_copy(slot).wait_send()
-        q_copy(slot).wait_send()
         sp_copy(slot).wait_send()
         po_copy(slot).wait_send()
         ps_copy(slot).wait_send()
@@ -409,24 +520,31 @@
     cache_lengths,
     owner_rows,
 ):
-    smem = pl.BlockSpec(memory_space=pltpu.SMEM)
     vmem = pl.BlockSpec(memory_space=pltpu.VMEM)
-    hbm = pl.BlockSpec(memory_space=pl.ANY)
+    hbm = pl.BlockSpec(memory_space=pltpu.HBM)
     sem = pltpu.SemaphoreType.DMA
     return pl.pallas_call(
         kernel,
         out_shape=(
-            jax.ShapeDtypeStruct(span_queries.shape, BF16),
-            jax.ShapeDtypeStruct(decode_queries.shape, BF16),
+            pltpu.VMEM(span_queries.shape, BF16),
+            pltpu.VMEM(decode_queries.shape, BF16),
         ),
-        in_specs=[smem, smem, smem, vmem, vmem, hbm, hbm, hbm],
+        in_specs=[hbm] * 8,
         out_specs=(vmem, vmem),
         scratch_shapes=[
+            pltpu.SMEM((1,), jnp.int32),
+            pltpu.SMEM((4,), jnp.int32),
+            pltpu.SMEM((4,), jnp.int32),
+            pltpu.VMEM((4, 512), BF16),
+            pltpu.VMEM((1, 2, 4, 1024), BF16),
             pltpu.VMEM((4, 2, 128, 1024), BF16),
             pltpu.VMEM((8, 2, 256, HEAD_DIM), BF16),
             pltpu.VMEM((HEAD_DIM, 2048), BF16),
             pltpu.VMEM((8, 64, 512), BF16),
             pltpu.VMEM((8, 256, 256), F32),
+            pltpu.VMEM((8, 8, 256), F32),
+            pltpu.VMEM((8, 8, 256), F32),
+            pltpu.VMEM((8, HEAD_DIM, 256), F32),
             pltpu.VMEM((8, HEAD_DIM, 256), BF16),
             pltpu.VMEM((8, HEAD_DIM, 256), BF16),
             pltpu.VMEM((8, 8, 256), F32),
@@ -434,7 +552,7 @@
             pltpu.VMEM((8, 8, HEAD_DIM), F32),
             pltpu.VMEM((8, 8, HEAD_DIM), F32),
             pltpu.VMEM((64, HEAD_DIM), BF16),
-            pltpu.VMEM((16, 64, HEAD_DIM), BF16),
+            pltpu.VMEM((2, 2, 4, 64, HEAD_DIM), BF16),
             pltpu.VMEM((16, 64, HEAD_DIM), F32),
             pltpu.VMEM((16, HEAD_DIM), F32),
             pltpu.VMEM((16, HEAD_DIM), BF16),
@@ -442,7 +560,7 @@
             pltpu.VMEM((16, 2, 16, HEAD_DIM), F32),
             pltpu.VMEM((16, 2, 16, HEAD_DIM), F32),
             pltpu.VMEM((16, HEAD_DIM), F32),
-            sem((3,)),
+            sem((8,)),
             sem((8,)),
             sem((8,)),
             sem((8,)),
@@ -461,7 +579,7 @@
             sem((8,)),
         ],
         compiler_params=pltpu.CompilerParams(
-            collective_id=0, has_side_effects=True, vmem_limit_bytes=48 * 1024 * 1024
+            collective_id=0, has_side_effects=True, vmem_limit_bytes=60 * 1024 * 1024
         ),
     )(
         span_offsets,

time: 60.6 us -> 51.2 us (0.84)
  the two profiles are of different devices: /device:TPU:39 before, /device:TPU:1 now
where the time goes in v2:
time: 51.2 us; the launch traced here: 51.1 us
  Pallas kernels  48.6 us (95%)
  between operations  1.29 us (3%)
  local copies, waits for them, and re-layouts  1.22 us (2%)
    pallas_call x1, Pallas kernels, body(): pl.pallas_call(kernel, out_shape=(pltpu.VMEM(span_queries.shape, BF16), p...  48.6 us
    unnamed x2, local copies, waits for them, and re-layouts  1.22 us

profile of v2, /device:TPU:1, one launch (start us, length us, event | category | flops | bytes accessed | tf_op | source)
XLA Modules:
  0.0 51.1 jit_solution(4886097488291427044)
XLA Ops:
  1.3 48.6 %shard_map.95 = (bf16[1,64,512]{2,1,0:T(8,128)(2,1)S(1)}, bf16[4,512]{1,0:T(4,128)(2,1)S(1)}) custom-call(s32[1]{0:T(128)S(6)} %copy.14.off_hbm, s32[4]{0:T(128)} %len_hbm.1, s32[4]{0:T(128)} %own_hbm.1, bf16[4,512]{1,0:T(4,128)(2,1)} %dq_hbm.1, bf16[1,2,4,1024]{3,2,1,0:T(4,128)(2,1)} %skv_hbm.1, bf16[1,64,512]{2,1,0:T(8,128)(2,1)} %q_hbm.1, ...), custom_call_target="tpu_custom_call" | custom-call | tf_op jit(solution)/shard_map/pallas_call | solution.py:526
  49.9 0.6 %copy.12 = bf16[1,64,512]{2,1,0:T(8,128)(2,1)} copy(bf16[1,64,512]{2,1,0:T(8,128)(2,1)S(1)} %get-tuple-element.2) | data formatting | bytes 131072
  50.5 0.6 %copy.13 = bf16[4,512]{1,0:T(4,128)(2,1)} copy(bf16[4,512]{1,0:T(4,128)(2,1)S(1)} %get-tuple-element.3) | data formatting | bytes 8192

commit v3 on v2

--- a/solution.py
+++ b/solution.py
@@ -54,6 +54,7 @@
     dq_ref,
     skv_ref,
     cache,
+    staged,
     kv,
     vt,
     q_all,
@@ -77,6 +78,7 @@
     dp_recv,
     d_result,
     local_sem,
+    stage_sem,
     kv_ssem,
     kv_rsem,
     q_ssem,
@@ -85,6 +87,8 @@
     sp_rsem,
     sa_ssem,
     sa_rsem,
+    ring_ssem,
+    ring_rsem,
     dq_ssem,
     dq_rsem,
     dp_ssem,
@@ -115,15 +119,10 @@
     core = s % 2
     layer = (s // 2) * 4 + c
 
-    def span_peer(step):
-        far = (layer + step) % 8
-        return (far // 4) * 2 + core, far % 4
-
     def kv_copy(slot):
         far = kv_peer(slot, 1)
-        column = pl.multiple_of((far // 2) * HEAD_DIM, HEAD_DIM)
-        return pltpu.make_async_remote_copy(
-            src_ref=pc_hbm.at[0, :, :, pl.ds(column, HEAD_DIM)],
+        return pltpu.make_async_remote_copy(
+            src_ref=staged.at[far // 2],
             dst_ref=kv.at[slot],
             send_sem=kv_ssem.at[slot],
             recv_sem=kv_rsem.at[slot],
@@ -133,7 +132,7 @@
 
     def q_copy(step):
         return pltpu.make_async_remote_copy(
-            src_ref=q_hbm.at[0],
+            src_ref=q_all.at[0],
             dst_ref=q_all.at[2 * step],
             send_sem=q_ssem.at[2 * step],
             recv_sem=q_rsem.at[2 * step],
@@ -162,23 +161,39 @@
             device_id_type=MESH,
         )
 
-    def sa_copy(step):
-        far_s, far_c = span_peer(step)
-        return pltpu.make_async_remote_copy(
-            src_ref=sp_block,
-            dst_ref=sp_all.at[s // 2, core, c],
-            send_sem=sa_ssem.at[step],
-            recv_sem=sa_rsem.at[step],
-            device_id=(far_s, far_c, t),
-            device_id_type=MESH,
-        )
+    def ring_peer(shift):
+        far = (layer + shift + 8) % 8
+        return (far // 4) * 2 + core, far % 4
+
+    ring_steps = (((0, 1), (0, -1), (0, 2), (0, -2)), ((1, -2), (2, -2), (-1, 2)))
+
+    def ring_copies(step):
+        for index, (block, shift) in enumerate(ring_steps[step]):
+            far_s, far_c = ring_peer(shift)
+            moved = (layer + block + 8) % 8
+            yield pltpu.make_async_remote_copy(
+                src_ref=sp_all.at[moved // 4, core, moved % 4],
+                dst_ref=sp_all.at[moved // 4, core, moved % 4],
+                send_sem=ring_ssem.at[4 * step + index],
+                recv_sem=ring_rsem.at[4 * step + index],
+                device_id=(far_s, far_c, t),
+                device_id_type=MESH,
+            )
+
+    def ring_start(step):
+        for copy in ring_copies(step):
+            copy.start()
+
+    def ring_wait(step):
+        for copy in ring_copies(step):
+            copy.wait_recv()
 
     def sa_forward():
         return pltpu.make_async_remote_copy(
             src_ref=sp_all.at[:, core],
             dst_ref=sp_all.at[:, core],
-            send_sem=sa_ssem.at[0],
-            recv_sem=sa_rsem.at[0],
+            send_sem=sa_ssem,
+            recv_sem=sa_rsem,
             device_id=(s + 1 - 2 * core, c, t),
             device_id_type=MESH,
         )
@@ -204,8 +219,12 @@
             device_id_type=MESH,
         )
 
+    def sum_peer(slot):
+        far_c, far_t = q_peer(slot, -1)
+        return jnp.where(slot == 5, c, far_c), far_t
+
     def po_copy(slot):
-        far_c, far_t = q_peer(slot, -1)
+        far_c, far_t = sum_peer(slot)
         return pltpu.make_async_remote_copy(
             src_ref=po_send.at[slot],
             dst_ref=po_recv.at[slot],
@@ -216,7 +235,7 @@
         )
 
     def ps_copy(slot):
-        far_c, far_t = q_peer(slot, -1)
+        far_c, far_t = sum_peer(slot)
         return pltpu.make_async_remote_copy(
             src_ref=ps_send.at[slot],
             dst_ref=ps_recv.at[slot],
@@ -233,12 +252,13 @@
             barrier, inc=1, device_id=(far_s, far_c, far_t), device_id_type=MESH
         )
 
-    for step in range(1, 8):
-        far_s, far_c = span_peer(step)
+    for shift in (2, -2, 1, -1):
+        far_s, far_c = ring_peer(shift)
         greet(far_s, far_c, t)
     for step in range(1, 16):
         greet(s, c, (t + step) % 16)
     for step in range(1, 4):
+        greet(s, (c + step) % 4, t)
         greet(s, (c + step) % 4, pair)
     greet(s + 1 - 2 * core, c, t)
 
@@ -263,6 +283,14 @@
     local_q = pltpu.make_async_copy(q_hbm.at[0], q_all.at[0], local_sem.at[1])
     local_cache = pltpu.make_async_copy(dc_hbm, cache, local_sem.at[2])
     local_q.start()
+    stage = [
+        pltpu.make_async_copy(
+            pc_hbm.at[0, :, :, h * HEAD_DIM : (h + 1) * HEAD_DIM], staged.at[h], stage_sem.at[h]
+        )
+        for h in range(8)
+    ]
+    for copy in stage:
+        copy.start()
     local_kv.start()
     local_cache.start()
 
@@ -282,11 +310,14 @@
     sp_all[s // 2, core, c] = sp_block[...]
     sp_pre[0] = sp_head[head]
     local_q.wait()
+    for copy in stage:
+        copy.wait()
 
     pl.semaphore_wait(barrier, 26)
 
     for step in range(1, 16):
         dq_copy(step).start()
+    ring_start(0)
     for slot in NEAR[1:]:
         kv_copy(slot).start()
     q_forward(0).start()
@@ -326,12 +357,14 @@
         return carry
 
     lax.fori_loop(0, 4, decode_cached, 0)
-    for step in (1, 3, 2):
+    for step in (1, 3):
         q_copy(step).wait_recv()
         q_forward(step).start()
-    for step in range(1, 8):
-        sa_copy(step).start()
     lax.fori_loop(4, 8, decode_cached, 0)
+    q_copy(2).wait_recv()
+    q_forward(2).start()
+    ring_wait(0)
+    ring_start(1)
 
     local_kv.wait()
     offset = off_ref[0]
@@ -367,7 +400,7 @@
     transpose_values(NEAR)
 
     def first_pass(i, carry):
-        slot = (i + 1) % 8
+        slot = (2 * i) % 8 + i // 4
 
         @pl.when(slot % 2 == 1)
         def _():
@@ -383,7 +416,10 @@
         run_acc[slot] = acc
         return carry
 
-    lax.fori_loop(0, 8, first_pass, 0)
+    lax.fori_loop(0, 4, first_pass, 0)
+    ring_wait(1)
+    sa_forward().start()
+    lax.fori_loop(4, 8, first_pass, 0)
 
     for slot in range(1, 8):
         sp_copy(slot).wait_recv()
@@ -400,8 +436,12 @@
     span_token = (c * 16 + span_y * 4 + span_x) * 4 + span_row % 8
     span_real = span_row % 8 < 4
 
+    def publish(slot, top, total, acc):
+        po_send[slot] = acc.astype(BF16)
+        ps_send[slot] = jnp.where(iota((8, 256), 0) < 4, top, total)
+
     def second_pass(i, carry):
-        slot = (i + 1) % 8
+        slot = (i + 5) % 8
         far_c, _ = q_peer(slot, -1)
         queries = load_queries(slot)
         span_live = span_real & (span_token <= far_c * 64 + iota((64, 256), 1) % 64)
@@ -414,21 +454,37 @@
         acc = run_acc[slot] * factor[0:1] + dot_nn(span_vt, weights.astype(BF16))
         total, acc = collect(FAR, top, total, acc)
         total = jnp.sum(total, axis=0, keepdims=True)
-        po_send[slot] = acc.astype(BF16)
-        ps_send[slot] = jnp.where(iota((8, 256), 0) < 4, top, total)
-
-        @pl.when(slot > 0)
+
+        @pl.when(slot != 4)
+        def _():
+            publish(slot, top, total, acc)
+
+        @pl.when((slot != 0) & (slot != 4))
         def _():
             po_copy(slot).start()
             ps_copy(slot).start()
 
+        @pl.when(slot == 4)
+        def _():
+            run_top[4] = jnp.broadcast_to(top, (8, 256))
+            run_total[4] = jnp.broadcast_to(total, (8, 256))
+            run_acc[4] = acc
+
         return carry
 
     lax.fori_loop(0, 8, second_pass, 0)
 
-    for step in range(1, 8):
-        sa_copy(step).wait_recv()
-    sa_forward().start()
+    def join(one, other):
+        top = jnp.maximum(one[0], other[0])
+        left = jnp.exp2((one[0] - top) * EXP2_SCALE)
+        right = jnp.exp2((other[0] - top) * EXP2_SCALE)
+        return top, one[1] * left + other[1] * right, one[2] * left + other[2] * right
+
+    def received(slot):
+        po_copy(slot).wait_recv()
+        ps_copy(slot).wait_recv()
+        return ps_recv[slot, 0:1, :], ps_recv[slot, 4:5, :], po_recv[slot].astype(F32)
+
     sa_forward().wait_recv()
     sp_wide[...] = sp_all[...].reshape(16, 64, HEAD_DIM).astype(F32)
     new_col = iota((32, 128), 1)
@@ -457,6 +513,14 @@
     lax.fori_loop(0, 8, decode_fresh, 0)
     for step in range(1, 16):
         dp_copy(step).start()
+
+    publish(4, *join((run_top[4, 0:1, :], run_total[4, 0:1, :], run_acc[4]), received(5)))
+    po_copy(4).start()
+    ps_copy(4).start()
+
+    state = (ps_send[0, 0:1, :], ps_send[0, 4:5, :], po_send[0].astype(F32))
+    for slot in (1, 6, 7, 2, 3):
+        state = join(state, received(slot))
 
     for step in range(1, 16):
         dp_copy(step).wait_recv()
@@ -475,20 +539,7 @@
     for h in range(4):
         dout_ref[:, h * HEAD_DIM : (h + 1) * HEAD_DIM] = d_result[4 * h : 4 * h + 4, :].astype(BF16)
 
-    for slot in range(1, 8):
-        ps_copy(slot).wait_recv()
-        po_copy(slot).wait_recv()
-    ps_recv[0] = ps_send[0]
-    po_recv[0] = po_send[0]
-    top = ps_recv[0, 0:1, :]
-    for i in range(1, 8):
-        top = jnp.maximum(top, ps_recv[i, 0:1, :])
-    acc = jnp.zeros((HEAD_DIM, 256), F32)
-    total = jnp.zeros((1, 256), F32)
-    for i in range(8):
-        factor = jnp.exp2((ps_recv[i, 0:1, :] - top) * EXP2_SCALE)
-        acc += po_recv[i].astype(F32) * factor
-        total += ps_recv[i, 4:5, :] * factor
+    _, total, acc = join(state, received(4))
     result = (acc / total).T
     for h in range(4):
         out_ref[0, :, h * HEAD_DIM : (h + 1) * HEAD_DIM] = result[h * 64 : (h + 1) * 64].astype(BF16)
@@ -500,8 +551,9 @@
         q_forward(step).wait_send()
     for step in range(1, 4):
         q_copy(step).wait_send()
-    for step in range(1, 8):
-        sa_copy(step).wait_send()
+    for step in range(2):
+        for copy in ring_copies(step):
+            copy.wait_send()
     sa_forward().wait_send()
     for slot in range(1, 8):
         kv_copy(slot).wait_send()
@@ -539,6 +591,7 @@
             pltpu.VMEM((1, 2, 4, 1024), BF16),
             pltpu.VMEM((4, 2, 128, 1024), BF16),
             pltpu.VMEM((8, 2, 256, HEAD_DIM), BF16),
+            pltpu.VMEM((8, 2, 256, HEAD_DIM), BF16),
             pltpu.VMEM((HEAD_DIM, 2048), BF16),
             pltpu.VMEM((8, 64, 512), BF16),
             pltpu.VMEM((8, 256, 256), F32),
@@ -567,8 +620,11 @@
             sem((8,)),
             sem((8,)),
             sem((8,)),
-            sem((16,)),
-            sem((16,)),
+            sem((8,)),
+            sem(()),
+            sem(()),
+            sem((8,)),
+            sem((8,)),
             sem((16,)),
             sem((16,)),
             sem((16,)),

time: 51.2 us -> 47 us (0.918)
  the two profiles are of different devices: /device:TPU:1 before, /device:TPU:2 now
where the time goes in v3:
time: 47 us; the launch traced here: 46.9 us
  Pallas kernels  44.4 us (94%)
  between operations  1.29 us (3%)
  local copies, waits for them, and re-layouts  1.22 us (3%)
    pallas_call x1, Pallas kernels, body(): pl.pallas_call(kernel, out_shape=(pltpu.VMEM(span_queries.shape, BF16), p...  44.4 us
    unnamed x2, local copies, waits for them, and re-layouts  1.22 us

profile of v3, /device:TPU:2, one launch (start us, length us, event | category | flops | bytes accessed | tf_op | source)
XLA Modules:
  0.0 46.9 jit_solution(14351849201291261665)
XLA Ops:
  1.3 44.4 %shard_map.95 = (bf16[1,64,512]{2,1,0:T(8,128)(2,1)S(1)}, bf16[4,512]{1,0:T(4,128)(2,1)S(1)}) custom-call(s32[1]{0:T(128)S(6)} %copy.14.off_hbm, s32[4]{0:T(128)} %len_hbm.1, s32[4]{0:T(128)} %own_hbm.1, bf16[4,512]{1,0:T(4,128)(2,1)} %dq_hbm.1, bf16[1,2,4,1024]{3,2,1,0:T(4,128)(2,1)} %skv_hbm.1, bf16[1,64,512]{2,1,0:T(8,128)(2,1)} %q_hbm.1, ...), custom_call_target="tpu_custom_call" | custom-call | tf_op jit(solution)/shard_map/pallas_call | solution.py:578
  45.6 0.6 %copy.12 = bf16[1,64,512]{2,1,0:T(8,128)(2,1)} copy(bf16[1,64,512]{2,1,0:T(8,128)(2,1)S(1)} %get-tuple-element.2) | data formatting | bytes 131072
  46.3 0.6 %copy.13 = bf16[4,512]{1,0:T(4,128)(2,1)} copy(bf16[4,512]{1,0:T(4,128)(2,1)S(1)} %get-tuple-element.3) | data formatting | bytes 8192

commit v4 on v3

--- a/solution.py
+++ b/solution.py
@@ -59,6 +59,7 @@
     vt,
     q_all,
     scores,
+    span_scores,
     run_top,
     run_total,
     run_acc,
@@ -375,20 +376,17 @@
             [block[:, h * HEAD_DIM : (h + 1) * HEAD_DIM] for h in range(4)], axis=0
         )
 
-    def attend(slots, queries, top):
-        for b in slots:
-            start = (c * 16 + kv_peer(b, -1)) * 256
-            part = dot_nt(kv[b, 0], queries)
-            part = jnp.where(start + iota((256, 256), 0) < offset, part, NEG)
-            scores[b] = part
-            top = jnp.maximum(top, jnp.max(part.reshape(32, 8, 256), axis=0))
-        return jnp.max(top, axis=0, keepdims=True)
-
-    def collect(slots, top, total, acc):
-        for b in slots:
-            weights = jnp.exp2((scores[b] - top) * EXP2_SCALE)
-            total += jnp.sum(weights.reshape(32, 8, 256), axis=0)
-            acc += dot_nn(vt[:, b * 256 : (b + 1) * 256], weights.astype(BF16))
+    def attend_block(b, queries, top, side):
+        start = (c * 16 + kv_peer(b, -1)) * 256
+        part = dot_nt(kv[b, 0], queries)
+        part = jnp.where(start + iota((256, 256), 0) < offset, part, NEG)
+        scores[side, b] = part
+        return jnp.maximum(top, jnp.max(part.reshape(32, 8, 256), axis=0))
+
+    def collect_block(b, top, total, acc, side):
+        weights = jnp.exp2((scores[side, b] - top) * EXP2_SCALE)
+        total += jnp.sum(weights.reshape(32, 8, 256), axis=0)
+        acc += dot_nn(vt[:, b * 256 : (b + 1) * 256], weights.astype(BF16))
         return total, acc
 
     def transpose_values(slots):
@@ -399,27 +397,43 @@
         kv_copy(slot).wait_recv()
     transpose_values(NEAR)
 
-    def first_pass(i, carry):
+    def first_queries(i):
         slot = (2 * i) % 8 + i // 4
 
         @pl.when(slot % 2 == 1)
         def _():
             q_forward(slot // 2).wait_recv()
 
-        queries = load_queries(slot)
-        top = attend(NEAR, queries, jnp.full((8, 256), NEG, F32))
-        total, acc = collect(
-            NEAR, top, jnp.zeros((8, 256), F32), jnp.zeros((HEAD_DIM, 256), F32)
-        )
+        return load_queries(slot)
+
+    def first_step(i, top, side, last=False):
+        slot = (2 * i) % 8 + i // 4
+        queries = None if last else first_queries(i + 1)
+        total, acc = jnp.zeros((8, 256), F32), jnp.zeros((HEAD_DIM, 256), F32)
+        later = jnp.full((8, 256), NEG, F32)
+        for b in NEAR:
+            if not last:
+                later = attend_block(b, queries, later, 1 - side)
+            total, acc = collect_block(b, top, total, acc, side)
         run_top[slot] = jnp.broadcast_to(top, (8, 256))
         run_total[slot] = total
         run_acc[slot] = acc
-        return carry
-
-    lax.fori_loop(0, 4, first_pass, 0)
+        return jnp.max(later, axis=0, keepdims=True)
+
+    def first_steps(i, top):
+        return first_step(2 * i + 1, first_step(2 * i, top, 0), 1)
+
+    top = jnp.full((8, 256), NEG, F32)
+    queries = load_queries(0)
+    for b in NEAR:
+        top = attend_block(b, queries, top, 0)
+    top = jnp.max(top, axis=0, keepdims=True)
+    top = lax.fori_loop(0, 2, first_steps, top)
     ring_wait(1)
     sa_forward().start()
-    lax.fori_loop(4, 8, first_pass, 0)
+    top = lax.fori_loop(2, 3, first_steps, top)
+    top = first_step(6, top, 0)
+    first_step(7, top, 1, last=True)
 
     for slot in range(1, 8):
         sp_copy(slot).wait_recv()
@@ -438,41 +452,60 @@
 
     def publish(slot, top, total, acc):
         po_send[slot] = acc.astype(BF16)
-        ps_send[slot] = jnp.where(iota((8, 256), 0) < 4, top, total)
-
-    def second_pass(i, carry):
+        row = iota((8, HEAD_DIM), 0)
+        tops = jnp.where(row % 2 == 0, top[:, :HEAD_DIM], top[:, HEAD_DIM:])
+        totals = jnp.where(row % 2 == 0, total[:, :HEAD_DIM], total[:, HEAD_DIM:])
+        ps_send[slot] = jnp.where(row < 2, tops, totals)
+
+    def span_live_at(slot):
+        far_c, _ = q_peer(slot, -1)
+        return span_real & (span_token <= far_c * 64 + iota((64, 256), 1) % 64)
+
+    def second_queries(i, side):
         slot = (i + 5) % 8
-        far_c, _ = q_peer(slot, -1)
         queries = load_queries(slot)
-        span_live = span_real & (span_token <= far_c * 64 + iota((64, 256), 1) % 64)
-        span_part = jnp.where(span_live, dot_nt(span_keys, queries), NEG)
-        top = jnp.max(span_part.reshape(8, 8, 256), axis=0)
-        top = attend(FAR, queries, jnp.maximum(top, run_top[slot]))
+        part = jnp.where(span_live_at(slot), dot_nt(span_keys, queries), NEG)
+        span_scores[side] = part
+        top = jnp.maximum(run_top[slot], jnp.max(part.reshape(8, 8, 256), axis=0))
+        return queries, top
+
+    def second_step(i, top, side, last=False):
+        slot = (i + 5) % 8
+        queries, later = (None, None) if last else second_queries(i + 1, 1 - side)
         factor = jnp.exp2((run_top[slot] - top) * EXP2_SCALE)
-        weights = jnp.where(span_live, jnp.exp2((span_part - top) * EXP2_SCALE), 0.0)
+        weights = jnp.exp2((span_scores[side] - top) * EXP2_SCALE)
+        weights = jnp.where(span_live_at(slot), weights, 0.0)
         total = run_total[slot] * factor + jnp.sum(weights.reshape(8, 8, 256), axis=0)
         acc = run_acc[slot] * factor[0:1] + dot_nn(span_vt, weights.astype(BF16))
-        total, acc = collect(FAR, top, total, acc)
+        for b in FAR:
+            if not last:
+                later = attend_block(b, queries, later, 1 - side)
+            total, acc = collect_block(b, top, total, acc, side)
         total = jnp.sum(total, axis=0, keepdims=True)
-
-        @pl.when(slot != 4)
-        def _():
-            publish(slot, top, total, acc)
-
-        @pl.when((slot != 0) & (slot != 4))
+        if last:
+            run_top[slot] = jnp.broadcast_to(top, (8, 256))
+            run_total[slot] = jnp.broadcast_to(total, (8, 256))
+            run_acc[slot] = acc
+            return None
+        publish(slot, top, total, acc)
+
+        @pl.when(slot != 0)
         def _():
             po_copy(slot).start()
             ps_copy(slot).start()
 
-        @pl.when(slot == 4)
-        def _():
-            run_top[4] = jnp.broadcast_to(top, (8, 256))
-            run_total[4] = jnp.broadcast_to(total, (8, 256))
-            run_acc[4] = acc
-
-        return carry
-
-    lax.fori_loop(0, 8, second_pass, 0)
+        return jnp.max(later, axis=0, keepdims=True)
+
+    def second_steps(i, top):
+        return second_step(2 * i + 1, second_step(2 * i, top, 0), 1)
+
+    queries, top = second_queries(0, 0)
+    for b in FAR:
+        top = attend_block(b, queries, top, 0)
+    top = jnp.max(top, axis=0, keepdims=True)
+    top = lax.fori_loop(0, 3, second_steps, top)
+    top = second_step(6, top, 0)
+    second_step(7, top, 1, last=True)
 
     def join(one, other):
         top = jnp.maximum(one[0], other[0])
@@ -480,10 +513,14 @@
         right = jnp.exp2((other[0] - top) * EXP2_SCALE)
         return top, one[1] * left + other[1] * right, one[2] * left + other[2] * right
 
+    def unpack(stats):
+        top = jnp.concatenate([stats[0:1], stats[1:2]], axis=1)
+        return top, jnp.concatenate([stats[2:3], stats[3:4]], axis=1)
+
     def received(slot):
         po_copy(slot).wait_recv()
         ps_copy(slot).wait_recv()
-        return ps_recv[slot, 0:1, :], ps_recv[slot, 4:5, :], po_recv[slot].astype(F32)
+        return unpack(ps_recv[slot]) + (po_recv[slot].astype(F32),)
 
     sa_forward().wait_recv()
     sp_wide[...] = sp_all[...].reshape(16, 64, HEAD_DIM).astype(F32)
@@ -518,7 +555,7 @@
     po_copy(4).start()
     ps_copy(4).start()
 
-    state = (ps_send[0, 0:1, :], ps_send[0, 4:5, :], po_send[0].astype(F32))
+    state = unpack(ps_send[0]) + (po_send[0].astype(F32),)
     for slot in (1, 6, 7, 2, 3):
         state = join(state, received(slot))
 
@@ -594,14 +631,15 @@
             pltpu.VMEM((8, 2, 256, HEAD_DIM), BF16),
             pltpu.VMEM((HEAD_DIM, 2048), BF16),
             pltpu.VMEM((8, 64, 512), BF16),
-            pltpu.VMEM((8, 256, 256), F32),
+            pltpu.VMEM((2, 8, 256, 256), F32),
+            pltpu.VMEM((2, 64, 256), F32),
             pltpu.VMEM((8, 8, 256), F32),
             pltpu.VMEM((8, 8, 256), F32),
             pltpu.VMEM((8, HEAD_DIM, 256), F32),
             pltpu.VMEM((8, HEAD_DIM, 256), BF16),
             pltpu.VMEM((8, HEAD_DIM, 256), BF16),
-            pltpu.VMEM((8, 8, 256), F32),
-            pltpu.VMEM((8, 8, 256), F32),
+            pltpu.VMEM((8, 8, HEAD_DIM), F32),
+            pltpu.VMEM((8, 8, HEAD_DIM), F32),
             pltpu.VMEM((8, 8, HEAD_DIM), F32),
             pltpu.VMEM((8, 8, HEAD_DIM), F32),
             pltpu.VMEM((64, HEAD_DIM), BF16),

time: 47 us -> 42.8 us (0.911)
  Pallas kernels: 44.4 us -> 40.2 us
    pallas_call x1, Pallas kernels: 44.4 us -> 40.2 us  [body(): pl.pallas_call(kernel, out_shape=(pltpu.VMEM(span_queries.shape, BF16), p...]
where the time goes in v4:
time: 42.8 us; the launch traced here: 42.7 us
  Pallas kernels  40.2 us (94%)
  between operations  1.29 us (3%)
  local copies, waits for them, and re-layouts  1.22 us (3%)
    pallas_call x1, Pallas kernels, body(): pl.pallas_call(kernel, out_shape=(pltpu.VMEM(span_queries.shape, BF16), p...  40.2 us
    unnamed x2, local copies, waits for them, and re-layouts  1.22 us

profile of v4, /device:TPU:2, one launch (start us, length us, event | category | flops | bytes accessed | tf_op | source)
XLA Modules:
  0.0 42.7 jit_solution(17582195613414933073)
XLA Ops:
  1.3 40.2 %shard_map.95 = (bf16[1,64,512]{2,1,0:T(8,128)(2,1)S(1)}, bf16[4,512]{1,0:T(4,128)(2,1)S(1)}) custom-call(s32[1]{0:T(128)S(6)} %copy.14.off_hbm, s32[4]{0:T(128)} %len_hbm.1, s32[4]{0:T(128)} %own_hbm.1, bf16[4,512]{1,0:T(4,128)(2,1)} %dq_hbm.1, bf16[1,2,4,1024]{3,2,1,0:T(4,128)(2,1)} %skv_hbm.1, bf16[1,64,512]{2,1,0:T(8,128)(2,1)} %q_hbm.1, ...), custom_call_target="tpu_custom_call" | custom-call | tf_op jit(solution)/shard_map/pallas_call | solution.py:615
  41.5 0.6 %copy.12 = bf16[1,64,512]{2,1,0:T(8,128)(2,1)} copy(bf16[1,64,512]{2,1,0:T(8,128)(2,1)S(1)} %get-tuple-element.2) | data formatting | bytes 131072
  42.1 0.6 %copy.13 = bf16[4,512]{1,0:T(4,128)(2,1)} copy(bf16[4,512]{1,0:T(4,128)(2,1)S(1)} %get-tuple-element.3) | data formatting | bytes 8192

commit v5 on v4

--- a/solution.py
+++ b/solution.py
@@ -76,6 +76,7 @@
     dq_block,
     dq_all,
     dp_send,
+    dp_out,
     dp_recv,
     d_result,
     local_sem,
@@ -212,7 +213,7 @@
     def dp_copy(step):
         far = (t + step) % 16
         return pltpu.make_async_remote_copy(
-            src_ref=dp_send.at[far],
+            src_ref=dp_out.at[far],
             dst_ref=dp_recv.at[step],
             send_sem=dp_ssem.at[step],
             recv_sem=dp_rsem.at[step],
@@ -357,11 +358,11 @@
         dp_send[pl.ds(2 * k, 2), 1] = jnp.where(left, top, total).reshape(2, 16, HEAD_DIM)
         return carry
 
-    lax.fori_loop(0, 4, decode_cached, 0)
+    lax.fori_loop(0, 4, decode_cached, 0, unroll=True)
     for step in (1, 3):
         q_copy(step).wait_recv()
         q_forward(step).start()
-    lax.fori_loop(4, 8, decode_cached, 0)
+    lax.fori_loop(4, 8, decode_cached, 0, unroll=True)
     q_copy(2).wait_recv()
     q_forward(2).start()
     ring_wait(0)
@@ -543,11 +544,18 @@
         total = stats[:, 64:65] * factor + jnp.sum(part, axis=1, keepdims=True)
         acc = dp_send[pl.ds(2 * k, 2), 0].reshape(32, HEAD_DIM) * factor
         acc += dot_nn(pltpu.roll(part, 4, axis=1).astype(BF16), fresh)
-        dp_send[pl.ds(2 * k, 2), 0] = acc.reshape(2, 16, HEAD_DIM)
-        dp_send[pl.ds(2 * k, 2), 1] = jnp.where(left, top, total).reshape(2, 16, HEAD_DIM)
+        dp_out[pl.ds(2 * k, 2), 0] = acc.astype(BF16).reshape(2, 16, HEAD_DIM)
+        pieces = jnp.zeros((32, HEAD_DIM), F32)
+        lane = iota((32, HEAD_DIM), 1) // 16
+        for first, value in ((0, top), (3, total)):
+            for index in range(first, first + 3):
+                piece = value.astype(BF16).astype(F32)
+                pieces = jnp.where(lane == index, piece, pieces)
+                value = value - piece
+        dp_out[pl.ds(2 * k, 2), 1] = pieces.astype(BF16).reshape(2, 16, HEAD_DIM)
         return carry
 
-    lax.fori_loop(0, 8, decode_fresh, 0)
+    lax.fori_loop(0, 8, decode_fresh, 0, unroll=True)
     for step in range(1, 16):
         dp_copy(step).start()
 
@@ -561,8 +569,10 @@
 
     for step in range(1, 16):
         dp_copy(step).wait_recv()
-    dp_recv[0] = dp_send[t]
-    tops = [dp_recv[i, 1][:, 0:1] for i in range(16)]
+    dp_recv[0] = dp_out[t]
+    stats = [dp_recv[i, 1].astype(F32) for i in range(16)]
+    tops = [v[:, 0:1] + v[:, 16:17] + v[:, 32:33] for v in stats]
+    totals = [v[:, 48:49] + v[:, 64:65] + v[:, 80:81] for v in stats]
     top = tops[0]
     for i in range(1, 16):
         top = jnp.maximum(top, tops[i])
@@ -570,8 +580,8 @@
     total = jnp.zeros((16, 1), F32)
     for i in range(16):
         factor = jnp.exp2((tops[i] - top) * EXP2_SCALE)
-        acc += dp_recv[i, 0] * factor
-        total += dp_recv[i, 1][:, 64:65] * factor
+        acc += dp_recv[i, 0].astype(F32) * factor
+        total += totals[i] * factor
     d_result[...] = acc / total
     for h in range(4):
         dout_ref[:, h * HEAD_DIM : (h + 1) * HEAD_DIM] = d_result[4 * h : 4 * h + 4, :].astype(BF16)
@@ -649,7 +659,8 @@
             pltpu.VMEM((16, HEAD_DIM), BF16),
             pltpu.VMEM((16, 16, HEAD_DIM), BF16),
             pltpu.VMEM((16, 2, 16, HEAD_DIM), F32),
-            pltpu.VMEM((16, 2, 16, HEAD_DIM), F32),
+            pltpu.VMEM((16, 2, 16, HEAD_DIM), BF16),
+            pltpu.VMEM((16, 2, 16, HEAD_DIM), BF16),
             pltpu.VMEM((16, HEAD_DIM), F32),
             sem((8,)),
             sem((8,)),

time: 42.8 us -> 41.6 us (0.972)
  Pallas kernels: 40.2 us -> 39 us
    pallas_call x1, Pallas kernels: 40.2 us -> 39 us  [body(): pl.pallas_call(kernel, out_shape=(pltpu.VMEM(span_queries.shape, BF16), p...]
where the time goes in v5:
time: 41.6 us; the launch traced here: 41.5 us
  Pallas kernels  39 us (94%)
  between operations  1.29 us (3%)
  local copies, waits for them, and re-layouts  1.22 us (3%)
    pallas_call x1, Pallas kernels, body(): pl.pallas_call(kernel, out_shape=(pltpu.VMEM(span_queries.shape, BF16), p...  39 us
    unnamed x2, local copies, waits for them, and re-layouts  1.22 us

profile of v5, /device:TPU:2, one launch (start us, length us, event | category | flops | bytes accessed | tf_op | source)
XLA Modules:
  0.0 41.5 jit_solution(7287798407163949891)
XLA Ops:
  1.3 39.0 %shard_map.95 = (bf16[1,64,512]{2,1,0:T(8,128)(2,1)S(1)}, bf16[4,512]{1,0:T(4,128)(2,1)S(1)}) custom-call(s32[1]{0:T(128)S(6)} %copy.14.off_hbm, s32[4]{0:T(128)} %len_hbm.1, s32[4]{0:T(128)} %own_hbm.1, bf16[4,512]{1,0:T(4,128)(2,1)} %dq_hbm.1, bf16[1,2,4,1024]{3,2,1,0:T(4,128)(2,1)} %skv_hbm.1, bf16[1,64,512]{2,1,0:T(8,128)(2,1)} %q_hbm.1, ...), custom_call_target="tpu_custom_call" | custom-call | tf_op jit(solution)/shard_map/pallas_call | solution.py:625
  40.3 0.6 %copy.12 = bf16[1,64,512]{2,1,0:T(8,128)(2,1)} copy(bf16[1,64,512]{2,1,0:T(8,128)(2,1)S(1)} %get-tuple-element.2) | data formatting | bytes 131072
  40.9 0.6 %copy.13 = bf16[4,512]{1,0:T(4,128)(2,1)} copy(bf16[4,512]{1,0:T(4,128)(2,1)S(1)} %get-tuple-element.3) | data formatting | bytes 8192

commit v6 on v5

--- a/solution.py
+++ b/solution.py
@@ -15,6 +15,7 @@
 BF16 = jnp.bfloat16
 NEAR = (0, 1, 2, 6, 3, 7)
 FAR = (4, 5)
+FAR_FIRST = (10, 9, 11, 6, 14, 8, 2, 5, 7, 13, 15, 1, 3, 4, 12)
 
 
 def dot_nt(a, b):
@@ -462,8 +463,12 @@
         far_c, _ = q_peer(slot, -1)
         return span_real & (span_token <= far_c * 64 + iota((64, 256), 1) % 64)
 
+    def second_slot(i):
+        late = jnp.where(i == 7, 4, 6 - i)
+        return jnp.where(i < 3, i + 5, jnp.where(i < 5, i - 1, late))
+
     def second_queries(i, side):
-        slot = (i + 5) % 8
+        slot = second_slot(i)
         queries = load_queries(slot)
         part = jnp.where(span_live_at(slot), dot_nt(span_keys, queries), NEG)
         span_scores[side] = part
@@ -471,7 +476,7 @@
         return queries, top
 
     def second_step(i, top, side, last=False):
-        slot = (i + 5) % 8
+        slot = second_slot(i)
         queries, later = (None, None) if last else second_queries(i + 1, 1 - side)
         factor = jnp.exp2((run_top[slot] - top) * EXP2_SCALE)
         weights = jnp.exp2((span_scores[side] - top) * EXP2_SCALE)
@@ -556,7 +561,7 @@
         return carry
 
     lax.fori_loop(0, 8, decode_fresh, 0, unroll=True)
-    for step in range(1, 16):
+    for step in FAR_FIRST:
         dp_copy(step).start()
 
     publish(4, *join((run_top[4, 0:1, :], run_total[4, 0:1, :], run_acc[4]), received(5)))
@@ -566,6 +571,11 @@
     state = unpack(ps_send[0]) + (po_send[0].astype(F32),)
     for slot in (1, 6, 7, 2, 3):
         state = join(state, received(slot))
+
+    _, total, acc = join(state, received(4))
+    result = (acc / total).T
+    for h in range(4):
+        out_ref[0, :, h * HEAD_DIM : (h + 1) * HEAD_DIM] = result[h * 64 : (h + 1) * 64].astype(BF16)
 
     for step in range(1, 16):
         dp_copy(step).wait_recv()
@@ -585,11 +595,6 @@
     d_result[...] = acc / total
     for h in range(4):
         dout_ref[:, h * HEAD_DIM : (h + 1) * HEAD_DIM] = d_result[4 * h : 4 * h + 4, :].astype(BF16)
-
-    _, total, acc = join(state, received(4))
-    result = (acc / total).T
-    for h in range(4):
-        out_ref[0, :, h * HEAD_DIM : (h + 1) * HEAD_DIM] = result[h * 64 : (h + 1) * 64].astype(BF16)
 
     for step in range(1, 16):
         dq_copy(step).wait_send()

time: 41.6 us -> 41.4 us (level)
  no operation moved by 1% of the time
where the time goes in v6:
time: 41.4 us; the launch traced here: 41.3 us
  Pallas kernels  38.8 us (94%)
  between operations  1.29 us (3%)
  local copies, waits for them, and re-layouts  1.22 us (3%)
    pallas_call x1, Pallas kernels, body(): pl.pallas_call(kernel, out_shape=(pltpu.VMEM(span_queries.shape, BF16), p...  38.8 us
    unnamed x2, local copies, waits for them, and re-layouts  1.22 us

profile of v6, /device:TPU:2, one launch (start us, length us, event | category | flops | bytes accessed | tf_op | source)
XLA Modules:
  0.0 41.3 jit_solution(8371891766243289443)
XLA Ops:
  1.3 38.8 %shard_map.95 = (bf16[1,64,512]{2,1,0:T(8,128)(2,1)S(1)}, bf16[4,512]{1,0:T(4,128)(2,1)S(1)}) custom-call(s32[1]{0:T(128)S(6)} %copy.14.off_hbm, s32[4]{0:T(128)} %len_hbm.1, s32[4]{0:T(128)} %own_hbm.1, bf16[4,512]{1,0:T(4,128)(2,1)} %dq_hbm.1, bf16[1,2,4,1024]{3,2,1,0:T(4,128)(2,1)} %skv_hbm.1, bf16[1,64,512]{2,1,0:T(8,128)(2,1)} %q_hbm.1, ...), custom_call_target="tpu_custom_call" | custom-call | tf_op jit(solution)/shard_map/pallas_call | solution.py:630
  40.1 0.6 %copy.12 = bf16[1,64,512]{2,1,0:T(8,128)(2,1)} copy(bf16[1,64,512]{2,1,0:T(8,128)(2,1)S(1)} %get-tuple-element.2) | data formatting | bytes 131072
  40.7 0.6 %copy.13 = bf16[4,512]{1,0:T(4,128)(2,1)} copy(bf16[4,512]{1,0:T(4,128)(2,1)S(1)} %get-tuple-element.3) | data formatting | bytes 8192
